TPU v7x, 32 devices: a whole 2x2x4 slice. The times are simulated.
32 devices in a mesh: fsdp: 4 (over x, core), ctx: 8 (over z, y).
Axes of the slice: x: 2, y: 2, z: 4, core: 2. Of those that a mesh axis runs over, the one named last changes fastest.
Arguments:
- query_branch: bfloat16 [4, 2048, 4096], P('fsdp', 'ctx'), may hold values from -6 to 6
- key_branch: bfloat16 [4, 2048, 4096], P('fsdp', 'ctx'), may hold values from -6 to 6
- value_branch: bfloat16 [4, 2048, 4096], P('fsdp', 'ctx'), may hold values from -6 to 6
- cotangent: bfloat16 [4, 2048, 4096], P('fsdp', 'ctx'), may hold values from -6 to 6
- quantized_weight_codes: int32 [4096, 4096], P('ctx', 'fsdp'), may hold values from 0 to 15
- scale_code_bytes: int32 [4096, 64], P('ctx', 'fsdp'), may hold values from 0 to 255
- row_scale_second: float32 [4096], P('ctx'), may hold values from 0.01 to 0.1
- filters: bfloat16 [256, 128], replicated, may hold values from -0.5 to 0.5
- channel_skip_weight: float32 [4096], replicated, may hold values from -6 to 6
- adapter_down_weight: bfloat16 [4096, 64], P('ctx'), may hold values from -0.09375 to 0.09375
- adapter_up_weight: bfloat16 [64, 4096], P(None, 'fsdp'), may hold values from -0.75 to 0.75
Outputs:
- output: bfloat16 [4, 2048, 4096], P('fsdp', 'ctx')
- grad_query: bfloat16 [4, 2048, 4096], P('fsdp', 'ctx')
- grad_key: bfloat16 [4, 2048, 4096], P('fsdp', 'ctx')
- grad_value: bfloat16 [4, 2048, 4096], P('fsdp', 'ctx')
- grad_down: bfloat16 [4096, 64], P('ctx')
- grad_up: bfloat16 [64, 4096], P(None, 'fsdp')
All inputs are finite; a program needn't handle non-finite values.
Results may differ from a plain program's by a relative error of at most 0.0067.
Values may be sent and summed in bfloat16 or wider, within the bound.
A program may use at most 256 MiB of HBM per device.

v0:
```python
import math

import jax
import jax.numpy as jnp
from jax import lax
from jax.sharding import PartitionSpec as P

QBLOCK = 64


normal_levels = (
    -1.0,
    -0.6961928009986877,
    -0.5250730514526367,
    -0.39491748809814453,
    -0.28444138169288635,
    -0.18477343022823334,
    -0.09105003625154495,
    0.0,
    0.07958029955625534,
    0.16093020141124725,
    0.24611230194568634,
    0.33791524171829224,
    0.44070982933044434,
    0.5626170039176941,
    0.7229568362236023,
    1.0,
)
adapter_scale = 0.25


def from_behind(shard, axis, by):
    count = lax.axis_size(axis)
    pairs = [(i, i + by) for i in range(count) if 0 <= i + by < count]
    return lax.ppermute(shard, axis, pairs)


def dequantize(quantized_weight_codes, scale_code_bytes, row_scale_second):
    levels = jnp.zeros(quantized_weight_codes.shape, jnp.float32)
    for number in range(16):
        levels = jnp.where(quantized_weight_codes == number, normal_levels[number], levels)
    absmax = row_scale_second[:, None] * (scale_code_bytes.astype(jnp.float32) + 1.0) / 256.0
    absmax = jnp.repeat(absmax, QBLOCK, axis=1)
    return (levels * absmax).astype(jnp.bfloat16)


def toeplitz(filter_taps, filter_len):
    groups = filter_taps.shape[0]
    padded = jnp.concatenate([filter_taps, jnp.zeros((groups, filter_len), filter_taps.dtype)], 1)
    repeated = jnp.tile(padded, (1, filter_len))[:, : filter_len * (2 * filter_len - 1)]
    return repeated.reshape(groups, filter_len, 2 * filter_len - 1)


def block_conv(extended, toep, filter_len):
    row_count = extended.shape[0] - (filter_len - 1)
    blocks = row_count // filter_len
    current = extended[:row_count].reshape(blocks, filter_len, -1)
    following = jnp.concatenate(
        [extended[filter_len:], jnp.zeros((1, extended.shape[1]), extended.dtype)], 0
    )
    following = following.reshape(blocks, filter_len, -1)[:, : filter_len - 1]
    windows = jnp.concatenate([current, following], 1)
    windows = windows.reshape(blocks, 2 * filter_len - 1, toep.shape[0], -1)
    result = jnp.einsum("gts,bsgk->btgk", toep, windows, preferred_element_type=jnp.float32)
    return result.reshape(row_count, -1)


def local(
    query_branch,
    key_branch,
    value_branch,
    cotangent,
    quantized_weight_codes,
    scale_code_bytes,
    row_scale_second,
    filters,
    channel_skip_weight,
    adapter_down_weight,
    adapter_up_weight,
):
    filter_len = filters.shape[1]
    queries = query_branch[0]
    output_gradient = cotangent[0]
    row_count, channels = queries.shape
    token_count = query_branch.shape[0] * row_count * lax.axis_size("ctx") * lax.axis_size("fsdp")
    multiplier = adapter_scale / math.sqrt(token_count)
    query_float = queries.astype(jnp.float32)
    key_float = key_branch[0].astype(jnp.float32)
    value_float = value_branch[0].astype(jnp.float32)
    mixed = (key_float * value_float).astype(jnp.bfloat16)
    before = from_behind(mixed[row_count - (filter_len - 1) :], "ctx", 1)
    ahead_toep = toeplitz(jnp.flip(filters, 1), filter_len)
    back_toep = toeplitz(filters, filter_len)
    gated = block_conv(
        jnp.concatenate([before, mixed], 0), ahead_toep, filter_len
    ) + channel_skip_weight * mixed.astype(jnp.float32)
    gated_signal = (query_float * gated).astype(jnp.bfloat16)
    local_piece = dequantize(quantized_weight_codes, scale_code_bytes, row_scale_second)
    local_rows, up_complete = (
        lax.all_gather(local_piece, "fsdp", axis=1, tiled=True),
        lax.all_gather(adapter_up_weight, "fsdp", axis=1, tiled=True),
    )
    backward_up_term = jnp.einsum(
        "td,rd->tr", output_gradient, up_complete, preferred_element_type=jnp.float32
    ).astype(jnp.bfloat16)
    weight_rows = lax.all_gather(local_rows, "ctx", axis=0, tiled=True)
    rank_rows = lax.all_gather(adapter_down_weight, "ctx", axis=0, tiled=True)
    output_total = jnp.dot(gated_signal, weight_rows, preferred_element_type=jnp.float32)
    down_sum = jnp.dot(gated_signal, rank_rows, preferred_element_type=jnp.float32)
    elementwise_product = jnp.einsum(
        "td,cd->tc", output_gradient, weight_rows, preferred_element_type=jnp.float32
    )
    elementwise_product = elementwise_product + adapter_scale * jnp.einsum(
        "tr,cr->tc", backward_up_term, rank_rows, preferred_element_type=jnp.float32
    )
    down_projection = down_sum.astype(jnp.bfloat16)
    output = (
        output_total
        + adapter_scale * jnp.dot(down_projection, up_complete, preferred_element_type=jnp.float32)
    ).astype(jnp.bfloat16)
    grad_query = (elementwise_product * gated).astype(jnp.bfloat16)
    grad_gated = (elementwise_product * query_float).astype(jnp.bfloat16)
    leading = jnp.concatenate(
        [jnp.zeros((filter_len, channels), jnp.bfloat16), grad_gated[: filter_len - 1]], 0
    )
    spill = block_conv(leading, back_toep, filter_len)
    arrived = from_behind(spill[1:], "ctx", -1)
    tail_rows = jnp.concatenate(
        [grad_gated, jnp.zeros((filter_len - 1, channels), jnp.bfloat16)], 0
    )
    local_grad = block_conv(tail_rows, back_toep, filter_len)
    local_grad = local_grad + jnp.concatenate(
        [jnp.zeros((row_count - filter_len + 1, channels), jnp.float32), arrived], 0
    )
    grad_mixed = local_grad + channel_skip_weight * grad_gated.astype(jnp.float32)
    grad_key = (grad_mixed * value_float).astype(jnp.bfloat16)
    grad_value = (grad_mixed * key_float).astype(jnp.bfloat16)
    term_down = multiplier * jnp.einsum(
        "tc,tr->cr", gated_signal, backward_up_term, preferred_element_type=jnp.float32
    )
    term_up = multiplier * jnp.einsum(
        "tr,td->rd", down_projection, output_gradient, preferred_element_type=jnp.float32
    )
    total_down = lax.psum(term_down, "fsdp")
    grad_down = lax.psum_scatter(total_down, "ctx", scatter_dimension=0, tiled=True)
    total_up = lax.psum(term_up, "ctx")
    grad_up = lax.psum_scatter(total_up, "fsdp", scatter_dimension=1, tiled=True)
    return (
        output[None],
        grad_query[None],
        grad_key[None],
        grad_value[None],
        grad_down.astype(jnp.bfloat16),
        grad_up.astype(jnp.bfloat16),
    )


def solution(mesh):
    return jax.shard_map(
        local,
        mesh=mesh,
        in_specs=(
            P("fsdp", "ctx", None),
            P("fsdp", "ctx", None),
            P("fsdp", "ctx", None),
            P("fsdp", "ctx", None),
            P("ctx", "fsdp"),
            P("ctx", "fsdp"),
            P("ctx"),
            P(),
            P(),
            P("ctx", None),
            P(None, "fsdp"),
        ),
        out_specs=(
            P("fsdp", "ctx", None),
            P("fsdp", "ctx", None),
            P("fsdp", "ctx", None),
            P("fsdp", "ctx", None),
            P("ctx", None),
            P(None, "fsdp"),
        ),
        check_vma=False,
    )
```

profile of v0, /device:TPU:0, one launch (start us, length us, event | category | flops | bytes accessed | tf_op | source)
XLA Modules:
  0.0 931.9 jit_solution(2897489533364673542)
XLA Ops:
  7.2 3.0 copy.29
  10.3 4.3 fusion.36
  14.7 37.3 %all-gather.3.cloned.1.call-done = bf16[512,4096]{0,1:T(8,128)(2,1)} async-done(((bf16[512,1024]{0,1:T(8,128)(2,1)}), bf16[512,4096]{0,1:T(8,128)(2,1)}) %all-gather.3.cloned.1.call-update) | async-done | bytes 4194320 | tf_op jit(solution)/shard_map/all_gather | solution.py:100
  52.1 3.0 fusion.11
  56.5 4.6 collective-permute-start
  64.5 41.7 %copy.62 = bf16[32,8,128,256]{3,1,2,0:T(8,128)(2,1)S(1)} copy(bf16[32,8,128,256]{3,2,1,0:T(8,128)(2,1)S(1)} %bitcast.101) | data formatting | bytes 33554432
  106.2 6.6 slice.54
  112.8 56.7 %reshape.84 = bf16[256,128,255,1]{2,1,0,3:T(8,128)(2,1)} reshape(bf16[256,32640]{1,0:T(8,128)(2,1)} %slice.54) | data formatting | bytes 33423360 | tf_op jit(solution)/shard_map/reshape | solution.py:51
  169.5 56.7 %reshape.76 = bf16[256,128,255]{2,1,0:T(8,128)(2,1)} reshape(bf16[256,32640]{1,0:T(8,128)(2,1)} %slice.54) | data formatting | bytes 33423360 | tf_op jit(solution)/shard_map/reshape | solution.py:51
  227.6 41.7 %copy.60 = bf16[32,8,128,256]{3,1,2,0:T(8,128)(2,1)S(1)} copy(bf16[32,8,128,256]{3,2,1,0:T(8,128)(2,1)S(1)} %bitcast.102) | data formatting | bytes 33554432
  269.3 6.6 slice.52
  275.9 56.7 %reshape.83 = bf16[256,128,255,1]{2,1,0,3:T(8,128)(2,1)} reshape(bf16[256,32640]{1,0:T(8,128)(2,1)} %slice.52) | data formatting | bytes 33423360 | tf_op jit(solution)/shard_map/reshape | solution.py:51
  332.6 3.1 concatenate.45
  335.8 4.2 copy.57
  340.0 7.0 all_gather.15
  347.0 65.1 %all_gather.14 = bf16[4096,64]{0,1:T(8,128)(2,1)S(1)} all-gather(bf16[512,64]{0,1:T(8,128)(2,1)S(1)} %copy-done.12), channel_id=1, replica_groups=mesh['fsdp'=4,'ctx'=8] {'ctx'}, dimensions={0}, use_global_device_ids=true | all-gather | bytes 589824 | tf_op jit(solution)/shard_map/all_gather | solution.py:107
  412.9 2.9 pad_maximum_fusion
  415.8 4.1 copy.23
  419.9 4.0 concatenate.44
  423.9 3.3 copy.25
  427.2 9.7 %fusion.19 = f32[2,128,256,16]{1,3,0,2:T(8,128)S(1)} fusion(bf16[256,128,255,1]{2,1,0,3:T(8,128)(2,1)} %reshape.83, bf16[2,128,256,16]{1,3,0,2:T(8,128)(2,1)} %copy.25, bf16[2,127,256,16]{1,3,2,0:T(8,128)(2,1)S(1)} %bitcast.105), kind=kOutput, calls=%fused_computation.35 | convolution fusion | flops 543129600 | bytes 25083904 | tf_op jit(solution)/shard_map/gts,bsgk->btgk/dot_general | solution.py:64
  436.9 2.2 copy.27
  439.0 2.2 copy.73
  441.3 5.7 copy.28
  446.9 274.1 %all-gather.5.cloned.1.call-done = bf16[4096,4096]{0,1:T(8,128)(2,1)} async-done(((bf16[512,4096]{0,1:T(8,128)(2,1)}), bf16[4096,4096]{0,1:T(8,128)(2,1)}) %all-gather.5.cloned.1.call-update) | async-done | bytes 33554448 | tf_op jit(solution)/shard_map/all_gather | solution.py:106
  721.0 17.2 %convolution_bitcast_fusion = f32[256,4096]{1,0:T(8,128)} fusion(bf16[4096,4096]{0,1:T(8,128)(2,1)} %all-gather.5.cloned.1.call-done, bf16[1,256,4096]{2,1,0:T(8,128)(2,1)S(1)} %copy-done), kind=kOutput, calls=%fused_computation.4 | convolution fusion | flops 8589934592 | bytes 39845888 | tf_op jit(solution)/shard_map/td,cd->tc/dot_general | solution.py:110
  738.2 6.7 fusion.29
  747.7 2.3 fusion.40
  750.1 2.3 copy.59
  752.4 2.8 concatenate.56.clone
  755.2 12.3 %convolution_bitcast_fusion.1 = f32[1,128,256,16]{1,3,2,0:T(8,128)} fusion(bf16[255,256,16]{0,2,1:T(8,128)(2,1)} %bitcast.111, bf16[256,128,255]{2,1,0:T(8,128)(2,1)} %reshape.76), kind=kOutput, calls=%fused_computation.47 | convolution fusion | flops 267386880 | bytes 20897792 | tf_op jit(solution)/shard_map/gts,bsgk->btgk/dot_general | solution.py:64
  767.5 3.5 slice.57
  771.0 3.0 copy.52
  775.4 2.4 convolution_convert_fusion
  779.3 17.7 %fusion.43 = f32[256,4096]{1,0:T(8,128)} fusion(bf16[256,4096]{1,0:T(8,128)(2,1)} %copy-done.6, bf16[4096,4096]{0,1:T(8,128)(2,1)} %all-gather.5.cloned.1.call-done), kind=kOutput, calls=%fused_computation.55 | convolution fusion | flops 8589934592 | bytes 39845888 | tf_op jit(solution)/shard_map/dot_general | solution.py:108
  797.0 4.1 copy.46
  801.0 4.0 concatenate.49
  805.0 3.3 copy.48
  810.0 4.2 copy.58
  814.2 9.9 %fusion.24 = f32[2,128,256,16]{1,3,0,2:T(8,128)S(1)} fusion(bf16[256,128,255,1]{2,1,0,3:T(8,128)(2,1)} %reshape.84, bf16[2,128,256,16]{1,3,0,2:T(8,128)(2,1)} %copy.48, bf16[2,127,256,16]{1,3,2,0:T(8,128)(2,1)} %bitcast.106), kind=kOutput, calls=%fused_computation.36 | convolution fusion | flops 543129600 | bytes 25083904 | tf_op jit(solution)/shard_map/gts,bsgk->btgk/dot_general | solution.py:64
  826.2 2.3 copy.72
  828.5 5.6 copy.53
  834.2 4.4 fusion.7
  838.6 6.5 fusion.30
  845.0 12.7 %reduce-scatter.3.cloned.1.call-done = f32[512,64]{0,1:T(8,128)} async-done(((f32[4096,64]{0,1:T(8,128)}), f32[512,64]{0,1:T(8,128)}) %reduce-scatter.3.cloned.1.call-update) | async-done | bytes 131088 | tf_op jit(solution)/shard_map/reduce_scatter | solution.py:145
  857.7 12.5 %all-reduce.9 = bf16[512,64]{0,1:T(8,128)(2,1)} all-reduce(f32[512,64]{0,1:T(8,128)} %reduce-scatter.3.cloned.1.call-done), channel_id=1, replica_groups=mesh['fsdp'=4,'ctx'=8] {'fsdp'}, use_global_device_ids=true, to_apply=%region_0.1 | all-reduce | flops 32768 | bytes 196608 | tf_op jit(solution)/shard_map/psum | solution.py:144
  870.2 13.9 %reduce-scatter.5.cloned.1.call-done = f32[64,1024]{1,0:T(8,128)} async-done(((f32[64,4096]{1,0:T(8,128)}), f32[64,1024]{1,0:T(8,128)}) %reduce-scatter.5.cloned.1.call-update) | async-done | bytes 262160 | tf_op jit(solution)/shard_map/reduce_scatter | solution.py:147
  884.1 41.1 %all-reduce.10 = bf16[64,1024]{1,0:T(8,128)(2,1)} all-reduce(f32[64,1024]{1,0:T(8,128)} %reduce-scatter.5.cloned.1.call-done), channel_id=1, replica_groups=mesh['fsdp'=4,'ctx'=8] {'ctx'}, use_global_device_ids=true, to_apply=%region_2.3 | all-reduce | flops 65536 | bytes 393216 | tf_op jit(solution)/shard_map/psum | solution.py:146
  (59 shorter events, 16.7 us)
Async XLA Ops:
  7.2 405.0 %copy-start = (bf16[1,256,4096]{2,1,0:T(8,128)(2,1)S(1)}, bf16[1,256,4096]{2,1,0:T(8,128)(2,1)}, u32[]{:S(2)}) copy-start(bf16[1,256,4096]{2,1,0:T(8,128)(2,1)} %param.14) | copy-start | bytes 6291460
  7.2 3.1 copy-start.14
  7.2 3.1 copy-start.15
  7.2 44.8 %all-gather.3.cloned.1.call-start = ((), (), s32[]{:S(2)}) async-start(), calls=%async_computation.2 | async-start | bytes 5242880 | tf_op jit(solution)/shard_map/all_gather | solution.py:100
  14.7 706.3 %all-gather.5.cloned.1.call-start = ((), (), s32[]{:S(2)}) async-start(), calls=%async_computation.3 | async-start | bytes 37748736 | tf_op jit(solution)/shard_map/all_gather | solution.py:106
  52.0 805.7 %reduce-scatter.3.cloned.1.call-start = ((), (), s32[]{:S(2)}) async-start(), calls=%async_computation.4 | async-start | bytes 1179648 | tf_op jit(solution)/shard_map/reduce_scatter | solution.py:145
  55.1 6.1 copy-start.3
  56.5 6.5 copy-start.10
  56.5 356.3 %collective-permute-start = (bf16[127,4096]{1,0:T(8,128)(2,1)}, bf16[127,4096]{1,0:T(8,128)(2,1)}, u32[]{:S(2)}, u32[]{:S(2)}) collective-permute-start(bf16[127,4096]{1,0:T(8,128)(2,1)} %slice.49), channel_id=1, source_target_pairs={{0,1},{1,2},{2,3},{3,4},{4,5},{5,6},{6,7},{8,9},{9,10},{10,11},{11... | collective-permute-start | bytes 3121160 | tf_op jit(solution)/shard_map/ppermute | solution.py:35
  335.8 4.2 copy-start.11
  335.8 11.2 %copy-start.12 = (bf16[512,64]{0,1:T(8,128)(2,1)S(1)}, bf16[512,64]{0,1:T(8,128)(2,1)}, u32[]{:S(2)}) copy-start(bf16[512,64]{0,1:T(8,128)(2,1)} %param.20) | copy-start | bytes 196612
  340.0 72.9 %copy-start.4 = (bf16[256,4096]{1,0:T(8,128)(2,1)S(1)}, bf16[256,4096]{1,0:T(8,128)(2,1)}, u32[]{:S(2)}) copy-start(bf16[256,4096]{1,0:T(8,128)(2,1)} %copy-done.3) | copy-start | bytes 6291460
  423.9 3.3 copy-start.7
  446.9 291.2 %copy-start.13 = (f32[4096]{0:T(1024)S(1)}, f32[4096]{0:T(1024)}, u32[]{:S(2)}) copy-start(f32[4096]{0:T(1024)} %param.19) | copy-start | bytes 49156
  721.0 17.2 %copy-start.5 = (bf16[256,4096]{1,0:T(8,128)(2,1)S(1)}, bf16[256,4096]{1,0:T(8,128)(2,1)}, u32[]{:S(2)}) copy-start(bf16[256,4096]{1,0:T(8,128)(2,1)} %copy-done.3) | copy-start | bytes 6291460
  721.0 17.2 %copy-start.9 = (f32[256,4096]{1,0:T(8,128)S(1)}, f32[256,4096]{1,0:T(8,128)}, u32[]{:S(2)}) copy-start(f32[256,4096]{1,0:T(8,128)} %copy.28) | copy-start | bytes 12582916
  744.9 1.3 copy-start.6
  746.2 1.5 copy-start.16
  747.7 136.4 %reduce-scatter.5.cloned.1.call-start = ((), (), s32[]{:S(2)}) async-start(), calls=%async_computation.5 | async-start | bytes 1310720 | tf_op jit(solution)/shard_map/reduce_scatter | solution.py:147
  774.0 64.6 %collective-permute-start.1 = (f32[127,4096]{1,0:T(8,128)}, f32[127,4096]{1,0:T(8,128)}, u32[]{:S(2)}, u32[]{:S(2)}) collective-permute-start(f32[127,4096]{1,0:T(8,128)} %copy.52), channel_id=1, source_target_pairs={{1,0},{2,1},{3,2},{4,3},{5,4},{6,5},{7,6},{9,8},{10,9},{11,10},{12... | collective-permute-start | bytes 6242312 | tf_op jit(solution)/shard_map/ppermute | solution.py:35
  805.0 3.3 copy-start.1
  834.2 4.4 copy-start.2
  834.2 4.4 copy-start.8
Sparse Core Ops, SparseCore 0:
  14.8 37.1 all-gather.2
  53.5 667.4 all-gather.4
  747.8 109.8 reduce-scatter.2
  860.2 23.8 reduce-scatter.4
where the time goes:
time: 936 us; the launch traced here: 932 us
  local copies, waits for them, and re-layouts  345 us (37%)
  waiting for transfers between devices  338 us (36%)
  blocking collectives  126 us (13%)
  matrix products  83.8 us (9%)
  other arithmetic  19.1 us (2%)
  between operations  14.2 us (2%)
    all_gather x1, waiting for transfers between devices, local(): weight_rows = lax.all_gather(local_rows, 'ctx', axis=0, tiled=True)  274 us
    reshape x3, local copies, waits for them, and re-layouts, toeplitz(): return repeated.reshape(groups, filter_len, 2 * filter_len - 1)  170 us
    unnamed x42, local copies, waits for them, and re-layouts  103 us
    all_gather x1, blocking collectives, local(): rank_rows = lax.all_gather(adapter_down_weight, 'ctx', axis=0, tiled=True)  65.1 us
    psum x1, blocking collectives, local(): total_up = lax.psum(term_up, 'ctx')  41.1 us
    all_gather x1, waiting for transfers between devices, local(): lax.all_gather(local_piece, 'fsdp', axis=1, tiled=True)  37.3 us
    dot_general x3, matrix products, block_conv(): jnp.einsum('gts,bsgk->btgk', toep, windows, preferred_element_type=jnp.fl...  31.8 us
  transfers between devices with their start and end apart: 6, of which 4 were waited for; matrix products, arithmetic and copies ran while one was open for 44% of the time, Pallas kernels for 0%

commit v1 on v0

v1 whole, which is shorter than its diff:
```python
import functools
import math

import jax
import jax.numpy as jnp
from jax import lax
from jax.experimental import pallas as pl
from jax.experimental.pallas import tpu as pltpu
from jax.sharding import PartitionSpec as P

QBLOCK = 64
LANES = 128
MESH = pl.DeviceIdType.MESH
VMEM_LIMIT = 56 * 1024 * 1024

normal_levels = (
    -1.0,
    -0.6961928009986877,
    -0.5250730514526367,
    -0.39491748809814453,
    -0.28444138169288635,
    -0.18477343022823334,
    -0.09105003625154495,
    0.0,
    0.07958029955625534,
    0.16093020141124725,
    0.24611230194568634,
    0.33791524171829224,
    0.44070982933044434,
    0.5626170039176941,
    0.7229568362236023,
    1.0,
)
adapter_scale = 0.25


def from_behind(shard, axis, by):
    count = lax.axis_size(axis)
    pairs = [(i, i + by) for i in range(count) if 0 <= i + by < count]
    return lax.ppermute(shard, axis, pairs)


def dequantize(quantized_weight_codes, scale_code_bytes, row_scale_second):
    levels = jnp.zeros(quantized_weight_codes.shape, jnp.float32)
    for number in range(16):
        levels = jnp.where(quantized_weight_codes == number, normal_levels[number], levels)
    absmax = row_scale_second[:, None] * (scale_code_bytes.astype(jnp.float32) + 1.0) / 256.0
    absmax = jnp.repeat(absmax, QBLOCK, axis=1)
    return (levels * absmax).astype(jnp.bfloat16)


def gather_kernel(line, own_ref, all_ref, local_sem, recv, sib_recv, z_send, y_send, x_send, sib_send):
    f, c = lax.axis_index("fsdp"), lax.axis_index("ctx")
    x, k, z, y = f // 2, f % 2, c // 2, c % 2
    half = own_ref.shape[0] // 2
    x_peer = (lax.rem(f + 2, 4), c)
    sibling = (f + 1 - 2 * k, c)
    y_peer = (f, c + 1 - 2 * y)
    z_up, z_down = (f, c + 2), (f, c - 2)

    def place(h, xx, yy, zz, kk):
        rows = pl.ds((2 * zz + yy) * (2 * half) + h * half, half)
        return all_ref.at[2 * xx + kk, rows, :]

    def copy(h, xx, yy, zz, send, arrive, to):
        block = place(h, xx, yy, zz, k)
        return pltpu.make_async_remote_copy(
            src_ref=block, dst_ref=block, send_sem=send, recv_sem=arrive,
            device_id=to, device_id_type=MESH,
        )

    def along_x(h, xx, yy, zz):
        return copy(h, xx, yy, zz, x_send.at[h, xx, yy, zz], recv.at[h, xx, yy, zz], x_peer)

    def along_y(h, xx, yy, zz):
        return copy(h, xx, yy, zz, y_send.at[h, xx, yy, zz], recv.at[h, xx, yy, zz], y_peer)

    def along_z(h, zz, up):
        return copy(
            h, x, y, zz, z_send.at[h, up, zz], recv.at[h, x, y, zz], z_up if up else z_down
        )

    def to_sibling(h, xx, yy, zz):
        return copy(h, xx, yy, zz, sib_send.at[h, xx, yy, zz], sib_recv.at[h, xx, yy, zz], sibling)

    def arrived(h, xx, yy, zz):
        along_x(h, xx, yy, zz).wait_recv()

    def places(step):
        yield z - step, z - step >= 0, True
        if step:
            yield z + step, z + step < line, False

    def first(step):
        for zz, there, upward in places(step):
            @pl.when(there)
            def _():
                for h in (0, 1):
                    if step:
                        arrived(h, x, y, zz)
                    if upward:
                        @pl.when(z + 1 < line)
                        def _():
                            along_z(h, zz, 1).start()
                    if not upward or step == 0:
                        @pl.when(z > 0)
                        def _():
                            along_z(h, zz, 0).start()
                along_y(0, x, y, zz).start()
                along_x(1, x, y, zz).start()
                for h in (0, 1):
                    to_sibling(h, x, y, zz).start()

    def second(step):
        for zz, there, _ in places(step):
            @pl.when(there)
            def _():
                along_x(0, x, y, zz).start()
                along_y(1, x, y, zz).start()
                arrived(0, x, 1 - y, zz)
                along_x(0, x, 1 - y, zz).start()
                arrived(1, 1 - x, y, zz)
                along_y(1, 1 - x, y, zz).start()
                to_sibling(0, x, 1 - y, zz).start()
                to_sibling(1, 1 - x, y, zz).start()

    def third(step):
        for zz, there, _ in places(step):
            @pl.when(there)
            def _():
                for other in (y, 1 - y):
                    arrived(0, 1 - x, other, zz)
                    to_sibling(0, 1 - x, other, zz).start()
                for other in (x, 1 - x):
                    arrived(1, other, 1 - y, zz)
                    to_sibling(1, other, 1 - y, zz).start()

    mine = pltpu.make_async_copy(
        own_ref, all_ref.at[f, pl.ds(c * (2 * half), 2 * half), :], local_sem
    )
    mine.start()
    barrier = pltpu.get_barrier_semaphore()
    for peer in (x_peer, y_peer, sibling):
        pl.semaphore_signal(barrier, inc=1, device_id=peer, device_id_type=MESH)

    @pl.when(z + 1 < line)
    def _():
        pl.semaphore_signal(barrier, inc=1, device_id=z_up, device_id_type=MESH)

    @pl.when(z > 0)
    def _():
        pl.semaphore_signal(barrier, inc=1, device_id=z_down, device_id_type=MESH)

    inside = jnp.logical_and(z > 0, z + 1 < line)

    @pl.when(inside)
    def _():
        pl.semaphore_wait(barrier, 5)

    @pl.when(jnp.logical_not(inside))
    def _():
        pl.semaphore_wait(barrier, 4)

    mine.wait()
    for step in range(line + 2):
        if step < line:
            first(step)
        if 1 <= step <= line:
            second(step - 1)
        if step >= 2:
            third(step - 2)

    def finish(zz, carry):
        for xx in (0, 1):
            for yy in (0, 1):
                for h in (0, 1):
                    to_sibling(h, xx, yy, zz).wait()
        for yy in (0, 1):
            along_x(0, x, yy, zz).wait_send()
        along_x(1, x, y, zz).wait_send()
        for xx in (0, 1):
            along_y(1, xx, y, zz).wait_send()
        along_y(0, x, y, zz).wait_send()
        for h in (0, 1):
            @pl.when(jnp.logical_and(zz <= z, z + 1 < line))
            def _():
                along_z(h, zz, 1).wait_send()

            @pl.when(jnp.logical_and(zz >= z, z > 0))
            def _():
                along_z(h, zz, 0).wait_send()
        return carry

    lax.fori_loop(0, line, finish, 0)


def gather_weight(piece, n_f, n_c):
    rows, columns = piece.shape
    line = n_c // 2
    blocks = (2, 2, 2, line)
    return pl.pallas_call(
        functools.partial(gather_kernel, line),
        out_shape=jax.ShapeDtypeStruct((n_f, n_c * rows, columns), piece.dtype),
        in_specs=[pl.BlockSpec(memory_space=pl.ANY)],
        out_specs=pl.BlockSpec(memory_space=pl.ANY),
        scratch_shapes=[
            pltpu.SemaphoreType.DMA,
            pltpu.SemaphoreType.DMA(blocks),
            pltpu.SemaphoreType.DMA(blocks),
            pltpu.SemaphoreType.DMA((2, 2, line)),
            pltpu.SemaphoreType.DMA(blocks),
            pltpu.SemaphoreType.DMA(blocks),
            pltpu.SemaphoreType.DMA(blocks),
        ],
        compiler_params=pltpu.CompilerParams(
            collective_id=0, has_side_effects=True, vmem_limit_bytes=VMEM_LIMIT
        ),
        cost_estimate=pl.CostEstimate(
            flops=0, bytes_accessed=16 * n_f * n_c * rows * columns, transcendentals=0
        ),
        name="gather_weight",
    )(piece)


def conv_blocks(base, windows):
    filters_here, width = base.shape
    taps = width // 2
    toep = jnp.concatenate(
        [
            pltpu.roll(
                jnp.broadcast_to(base[g : g + 1], (taps, width)), 0, 1, stride=1, stride_axis=0
            )
            for g in range(filters_here)
        ],
        0,
    ).astype(jnp.bfloat16)
    product = jnp.dot(toep, jnp.concatenate(windows, 1), preferred_element_type=jnp.float32)
    lanes = lax.broadcasted_iota(jnp.int32, (taps, LANES), 1) // (LANES // filters_here)
    results = []
    for b in range(len(windows)):
        part = product[:, b * LANES : (b + 1) * LANES]
        chosen = part[:taps]
        for g in range(1, filters_here):
            chosen = jnp.where(lanes == g, part[g * taps : (g + 1) * taps], chosen)
        results.append(chosen)
    return jnp.concatenate(results, 0)


def ahead_kernel(query_ref, key_ref, value_ref, before_ref, base_ref, skip_ref, gated_ref, input_ref):
    taps = base_ref.shape[1] // 2
    mixed = (key_ref[...].astype(jnp.float32) * value_ref[...].astype(jnp.float32)).astype(
        jnp.bfloat16
    )
    joined = jnp.concatenate([before_ref[...], mixed], 0)
    windows = [joined[b * taps : (b + 2) * taps] for b in range(mixed.shape[0] // taps)]
    gated = conv_blocks(base_ref[...], windows) + skip_ref[...] * mixed.astype(jnp.float32)
    gated_ref[...] = gated
    input_ref[...] = (query_ref[...].astype(jnp.float32) * gated).astype(jnp.bfloat16)


def back_kernel(grad_ref, after_ref, key_ref, value_ref, base_ref, skip_ref, gk_ref, gv_ref):
    taps = base_ref.shape[1] // 2
    grad = grad_ref[...]
    joined = jnp.concatenate([grad, after_ref[...]], 0)
    windows = [joined[b * taps : (b + 2) * taps] for b in range(grad.shape[0] // taps)]
    grad_mixed = conv_blocks(base_ref[...], windows) + skip_ref[...] * grad.astype(jnp.float32)
    gk_ref[...] = (grad_mixed * value_ref[...].astype(jnp.float32)).astype(jnp.bfloat16)
    gv_ref[...] = (grad_mixed * key_ref[...].astype(jnp.float32)).astype(jnp.bfloat16)


def tile_call(kernel, operands, out_types, groups, name):
    rows, channels = operands[0].shape
    tiles = channels // LANES

    def spec(array):
        if array.shape[0] == groups:
            if array.shape[1] != channels:
                return pl.BlockSpec((groups // tiles, array.shape[1]), lambda i: (i, 0))
        return pl.BlockSpec((array.shape[0], LANES), lambda i: (0, i))

    return pl.pallas_call(
        kernel,
        grid=(tiles,),
        in_specs=[spec(a) for a in operands],
        out_specs=[pl.BlockSpec((rows, LANES), lambda i: (0, i)) for _ in out_types],
        out_shape=[jax.ShapeDtypeStruct((rows, channels), t) for t in out_types],
        compiler_params=pltpu.CompilerParams(vmem_limit_bytes=VMEM_LIMIT),
        cost_estimate=pl.CostEstimate(
            flops=rows * channels * 4096, bytes_accessed=rows * channels * 12, transcendentals=0
        ),
        name=name,
    )(*operands)


def product_kernel(
    weight_ref, cot_ref, input_ref, gated_ref, query_ref, back_up_ref, down_ref, proj_ref, up_ref,
    out_ref, gq_ref, gg_ref, total,
):
    step = pl.program_id(0)
    parts, _, width = weight_ref.shape

    @pl.when(step == 0)
    def _():
        total[...] = adapter_scale * jnp.dot(
            proj_ref[...], up_ref[...], preferred_element_type=jnp.float32
        )

    nt = (((1,), (1,)), ((), ()))
    back = adapter_scale * lax.dot_general(
        back_up_ref[...], down_ref[...], nt, preferred_element_type=jnp.float32
    )
    for f in range(parts):
        columns = slice(f * width, (f + 1) * width)
        weight = weight_ref[f]
        back = back + lax.dot_general(
            cot_ref[:, columns], weight, nt, preferred_element_type=jnp.float32
        )
        total[:, columns] += jnp.dot(input_ref[...], weight, preferred_element_type=jnp.float32)
    gq_ref[...] = (back * gated_ref[...]).astype(jnp.bfloat16)
    gg_ref[...] = (back * query_ref[...].astype(jnp.float32)).astype(jnp.bfloat16)

    @pl.when(step == pl.num_programs(0) - 1)
    def _():
        out_ref[...] = total[...].astype(jnp.bfloat16)


def products(weight, cot, gated_input, gated, query, back_up, down, proj, up):
    parts, channels, width = weight.shape
    rows = cot.shape[0]
    features = parts * width
    rank = down.shape[1]
    block = 512
    whole = lambda i: (0, 0)
    tile = pl.BlockSpec((rows, block), lambda i: (0, i))
    return pl.pallas_call(
        product_kernel,
        grid=(channels // block,),
        in_specs=[
            pl.BlockSpec((parts, block, width), lambda i: (0, i, 0)),
            pl.BlockSpec((rows, features), whole),
            tile,
            tile,
            tile,
            pl.BlockSpec((rows, rank), whole),
            pl.BlockSpec((block, rank), lambda i: (i, 0)),
            pl.BlockSpec((rows, rank), whole),
            pl.BlockSpec((rank, features), whole),
        ],
        out_specs=[pl.BlockSpec((rows, features), whole), tile, tile],
        out_shape=[
            jax.ShapeDtypeStruct((rows, features), jnp.bfloat16),
            jax.ShapeDtypeStruct((rows, channels), jnp.bfloat16),
            jax.ShapeDtypeStruct((rows, channels), jnp.bfloat16),
        ],
        scratch_shapes=[pltpu.VMEM((rows, features), jnp.float32)],
        compiler_params=pltpu.CompilerParams(vmem_limit_bytes=VMEM_LIMIT),
        cost_estimate=pl.CostEstimate(
            flops=4 * rows * channels * features,
            bytes_accessed=2 * channels * features,
            transcendentals=0,
        ),
        name="products",
    )(weight, cot, gated_input, gated, query, back_up, down, proj, up)


def local(
    query_branch,
    key_branch,
    value_branch,
    cotangent,
    quantized_weight_codes,
    scale_code_bytes,
    row_scale_second,
    filters,
    channel_skip_weight,
    adapter_down_weight,
    adapter_up_weight,
):
    groups, filter_len = filters.shape
    query, key, value, cot = query_branch[0], key_branch[0], value_branch[0], cotangent[0]
    row_count = query.shape[0]
    n_f, n_c = lax.axis_size("fsdp"), lax.axis_size("ctx")
    token_count = query_branch.shape[0] * row_count * n_c * n_f
    multiplier = adapter_scale / math.sqrt(token_count)
    skip = channel_skip_weight[None]

    tail = row_count - filter_len
    mixed_tail = (
        key[tail:].astype(jnp.float32) * value[tail:].astype(jnp.float32)
    ).astype(jnp.bfloat16)
    before = from_behind(mixed_tail, "ctx", 1)
    piece = dequantize(quantized_weight_codes, scale_code_bytes, row_scale_second)
    up = lax.all_gather(adapter_up_weight, "fsdp", axis=1, tiled=True)
    down = lax.all_gather(adapter_down_weight, "ctx", axis=0, tiled=True)
    taps = filters.astype(jnp.float32)
    zeros = jnp.zeros((groups, filter_len), jnp.float32)
    back_base = jnp.concatenate([taps, zeros], 1)
    ahead_base = jnp.concatenate([zeros[:, :1], jnp.flip(taps, 1), zeros[:, 1:]], 1)

    weight = gather_weight(piece, n_f, n_c)
    gated, gated_input = tile_call(
        ahead_kernel,
        (query, key, value, before, ahead_base, skip),
        (jnp.float32, jnp.bfloat16),
        groups,
        "conv_ahead",
    )
    back_up = lax.dot_general(
        cot, up, (((1,), (1,)), ((), ())), preferred_element_type=jnp.float32
    ).astype(jnp.bfloat16)
    proj = jnp.dot(gated_input, down, preferred_element_type=jnp.float32).astype(jnp.bfloat16)
    over_rows = (((0,), (0,)), ((), ()))
    term_down = lax.dot_general(
        gated_input, back_up, over_rows, preferred_element_type=jnp.float32
    )
    term_up = lax.dot_general(proj, cot, over_rows, preferred_element_type=jnp.float32)
    part_down = lax.psum_scatter(term_down, "ctx", scatter_dimension=0, tiled=True)
    part_up = lax.psum_scatter(term_up, "fsdp", scatter_dimension=1, tiled=True)
    grad_down = multiplier * lax.psum(part_down, "fsdp")
    grad_up = multiplier * lax.psum(part_up, "ctx")

    output, grad_query, grad_gated = products(
        weight, cot, gated_input, gated, query, back_up, down, proj, up
    )
    after = from_behind(grad_gated[:filter_len], "ctx", -1)
    grad_key, grad_value = tile_call(
        back_kernel,
        (grad_gated, after, key, value, back_base, skip),
        (jnp.bfloat16, jnp.bfloat16),
        groups,
        "conv_back",
    )
    return (
        output[None],
        grad_query[None],
        grad_key[None],
        grad_value[None],
        grad_down.astype(jnp.bfloat16),
        grad_up.astype(jnp.bfloat16),
    )


def solution(mesh):
    return jax.shard_map(
        local,
        mesh=mesh,
        in_specs=(
            P("fsdp", "ctx", None),
            P("fsdp", "ctx", None),
            P("fsdp", "ctx", None),
            P("fsdp", "ctx", None),
            P("ctx", "fsdp"),
            P("ctx", "fsdp"),
            P("ctx"),
            P(),
            P(),
            P("ctx", None),
            P(None, "fsdp"),
        ),
        out_specs=(
            P("fsdp", "ctx", None),
            P("fsdp", "ctx", None),
            P("fsdp", "ctx", None),
            P("fsdp", "ctx", None),
            P("ctx", None),
            P(None, "fsdp"),
        ),
        check_vma=False,
    )
```

time: 936 us -> 444 us (0.47)
  local copies, waits for them, and re-layouts: 345 us -> 5.49 us
  Pallas kernels: 0 us -> 266 us
  waiting for transfers between devices: 338 us -> 90.1 us
  blocking collectives: 126 us -> 40.3 us
  matrix products: 83.8 us -> 6.05 us
    all_gather x2 -> x0, waiting for transfers between devices: 311 us -> none  [the longest x1 274 us: local(): weight_rows = lax.all_gather(local_rows, 'ctx', axis=0, tiled=True)]
    pallas_call x0 -> x4, Pallas kernels: none -> 266 us  [the longest x1 193 us: gather_weight(): pl.pallas_call(functools.partial(gather_kernel, line), out_shape=jax.Shap...]
    reshape x5 -> x1, local copies, waits for them, and re-layouts: 182 us -> 1.81 us  [dequantize(): absmax = jnp.repeat(absmax, QBLOCK, axis=1)]
    unnamed x42 -> x27, local copies, waits for them, and re-layouts: 103 us -> 1.16 us
    dot_general x11 -> x4, matrix products: 83.8 us -> 6.05 us  [the longest x1 3.12 us: local(): lax.dot_general(gated_input, back_up, over_rows, preferred_element_type=j...]
    psum x0 -> x2, waiting for transfers between devices: none -> 57.7 us  [the longest x1 57.7 us: local(): grad_up = multiplier * lax.psum(part_up, 'ctx')]
    psum x2 -> x0, blocking collectives: 53.6 us -> none  [the longest x1 41.1 us: local(): total_up = lax.psum(term_up, 'ctx')]
    ppermute x2, waiting for transfers between devices: 0.01 us -> 32.3 us  [from_behind(): return lax.ppermute(shard, axis, pairs)]
  transfers between devices with their start and end apart: 6 -> 6, of which waited for: 4 -> 3; matrix products, arithmetic and copies ran while one was open for 44% -> 3% of each run, Pallas kernels for 0% -> 55%
where the time goes in v1:
time: 444 us; the launch traced here: 440 us
  Pallas kernels  266 us (60%)
  waiting for transfers between devices  90.1 us (20%)
  blocking collectives  40.3 us (9%)
  between operations  14 us (3%)
  other arithmetic  10.6 us (2%)
  starting transfers between devices  7.31 us (2%)
  matrix products  6.05 us (1%)
  local copies, waits for them, and re-layouts  5.49 us (1%)
    pallas_call x1, Pallas kernels, gather_weight(): pl.pallas_call(functools.partial(gather_kernel, line), out_shape=jax.Shap...  193 us
    psum x1, waiting for transfers between devices, local(): grad_up = multiplier * lax.psum(part_up, 'ctx')  57.7 us
    pallas_call x2, Pallas kernels, tile_call(): pl.pallas_call(kernel, grid=(tiles,), in_specs=[spec(a) for a in operands...  47.2 us
    all_gather x1, blocking collectives, local(): down = lax.all_gather(adapter_down_weight, 'ctx', axis=0, tiled=True)  33.2 us
    ppermute x2, waiting for transfers between devices, from_behind(): return lax.ppermute(shard, axis, pairs)  32.3 us
    pallas_call x1, Pallas kernels, products(): pl.pallas_call(product_kernel, grid=(channels // block,), in_specs=[pl.Bl...  26.3 us
  transfers between devices with their start and end apart: 6, of which 3 were waited for; matrix products, arithmetic and copies ran while one was open for 3% of the time, Pallas kernels for 55%

profile of v1, /device:TPU:0, one launch (start us, length us, event | category | flops | bytes accessed | tf_op | source)
XLA Modules:
  0.0 440.2 jit_solution(10126177929841189239)
XLA Ops:
  7.2 0.0 copy-start.2
  7.2 0.0 reduce-scatter.3.cloned.1.call-start
  7.2 1.9 fusion.4
  9.2 5.9 %collective-permute-start = (bf16[128,4096]{1,0:T(8,128)(2,1)S(1)}, bf16[128,4096]{1,0:T(8,128)(2,1)}, u32[]{:S(2)}, u32[]{:S(2)}) collective-permute-start(bf16[128,4096]{1,0:T(8,128)(2,1)S(1)} %fusion.4), channel_id=1, source_target_pairs={{0,1},{1,2},{2,3},{3,4},{4,5},{5,6},{6,7},{8,9},{9,10},{10,11},{11... | collective-permute-start | bytes 3145736 | tf_op jit(solution)/shard_map/ppermute | solution.py:40
  15.1 0.0 copy-done.5
  15.1 0.2 rev.4
  15.2 0.1 pad.3.clone
  15.3 7.2 %all_gather.6.up_ref = bf16[64,4096]{1,0:T(8,128)(2,1)S(1)} all-gather(bf16[64,1024]{1,0:T(8,128)(2,1)S(1)} %copy-done.7), channel_id=1, replica_groups=mesh['fsdp'=4,'ctx'=8] {'fsdp'}, dimensions={1}, use_global_device_ids=true | all-gather | bytes 655360 | tf_op jit(solution)/shard_map/all_gather | solution.py:393
  22.5 0.9 maximum_maximum_fusion.base_ref
  23.3 0.7 fusion.6.back_up_ref
  24.0 0.0 copy-start.9
  24.1 12.4 %collective-permute-done.before_ref = bf16[128,4096]{1,0:T(8,128)(2,1)} collective-permute-done((bf16[128,4096]{1,0:T(8,128)(2,1)S(1)}, bf16[128,4096]{1,0:T(8,128)(2,1)}, u32[]{:S(2)}, u32[]{:S(2)}) %collective-permute-start) | collective-permute-done | bytes 1048608 | tf_op jit(solution)/shard_map/ppermute | solution.py:40
  36.5 23.7 %conv_ahead.1 = (f32[256,4096]{1,0:T(8,128)}, bf16[256,4096]{1,0:T(8,128)(2,1)}) custom-call(bf16[256,4096]{1,0:T(8,128)(2,1)} %bitcast.29, bf16[256,4096]{1,0:T(8,128)(2,1)} %bitcast.25, bf16[256,4096]{1,0:T(8,128)(2,1)} %bitcast.27, bf16[128,4096]{1,0:T(8,128)(2,1)} %collective-permute-done.before_ref, f32[256,256]{1,0:T(8,128)} %maximum_maximum_fusion.base_ref, ...), custom_call_target="tpu_custom_call" | custom-call | flops 4294967296 | bytes 12582912 | tf_op jit(solution)/shard_map/conv_ahead/pallas_call | solution.py:281
  60.1 0.0 copy-start.8
  60.2 0.0 copy-start.10
  60.2 0.0 copy-start.11
  60.2 3.1 fusion.9
  63.3 0.0 reduce-scatter.3.cloned.1.call-update
  63.3 0.0 reduce-scatter.5.cloned.1.call-start
  63.4 0.0 copy-done.8
  63.4 0.1 copy.23
  63.6 0.2 broadcast_in_dim.86
  63.8 1.8 copy.21
  65.6 4.6 %multiply_convert_fusion.1.own_ref = bf16[512,1024]{1,0:T(8,128)(2,1)} fusion(f32[512,1024]{1,0:T(8,128)} %copy.21, s32[512,1024]{1,0:T(8,128)} %param.15), kind=kLoop, calls=%fused_computation.1 | loop fusion | flops 17825792 | bytes 5242880 | tf_op jit(solution)/shard_map/convert_element_type | solution.py:49
  70.3 192.9 %gather_weight.1.weight_ref = bf16[4,4096,1024]{2,1,0:T(8,128)(2,1)} custom-call(bf16[512,1024]{1,0:T(8,128)(2,1)} %multiply_convert_fusion.1.own_ref), custom_call_target="tpu_custom_call" | custom-call | bytes 268435456 | tf_op jit(solution)/shard_map/gather_weight/pallas_call | solution.py:201
  263.2 0.0 copy-start.3
  263.2 33.2 %all_gather.7.down_ref = bf16[4096,64]{1,0:T(8,128)(2,1)S(1)} all-gather(bf16[512,64]{1,0:T(8,128)(2,1)S(1)} %copy.23), channel_id=1, replica_groups=mesh['fsdp'=4,'ctx'=8] {'ctx'}, dimensions={0}, use_global_device_ids=true | all-gather | bytes 589824 | tf_op jit(solution)/shard_map/all_gather | solution.py:394
  296.3 0.0 copy-done
  296.4 0.7 fusion.8.proj_ref
  297.1 0.0 copy-done.3
  297.1 0.0 copy-start.6
  297.1 1.5 fusion
  298.6 0.0 reduce-scatter.5.cloned.1.call-update
  298.7 0.0 all-reduce.4.cloned.1.call-start
  298.7 26.3 %products.1 = (bf16[256,4096]{1,0:T(8,128)(2,1)}, bf16[256,4096]{1,0:T(8,128)(2,1)}, bf16[256,4096]{1,0:T(8,128)(2,1)}) custom-call(bf16[4,4096,1024]{2,1,0:T(8,128)(2,1)} %gather_weight.1.weight_ref, bf16[256,4096]{1,0:T(8,128)(2,1)} %bitcast.24, bf16[256,4096]{1,0:T(8,128)(2,1)} %get-tuple-element.13.input_ref, f32[256,4096]{1,0:T(8,128)} %get-tuple-element.14.gated_ref, ...), custom_call_target="tpu_custom_call" | custom-call | flops 17179869184 | bytes 33554432 | tf_op jit(solution)/shard_map/products/pallas_call | solution.py:335
  325.0 1.3 slice.21
  326.3 1.3 collective-permute-start.1
  327.6 0.0 reduce-scatter.3.cloned.1.call-done
  327.6 0.0 all-reduce.4.cloned.1.call-update
  327.7 0.0 all-reduce.6.cloned.1.call-start
  327.7 0.7 concatenate.7.base_ref
  328.4 0.0 all-reduce.6.cloned.1.call-update
  328.5 19.9 %collective-permute-done.1.after_ref = bf16[128,4096]{1,0:T(8,128)(2,1)S(1)} collective-permute-done((bf16[128,4096]{1,0:T(8,128)(2,1)S(1)}, bf16[128,4096]{1,0:T(8,128)(2,1)S(1)}, u32[]{:S(2)}, u32[]{:S(2)}) %collective-permute-start.1) | collective-permute-done | bytes 1048608 | tf_op jit(solution)/shard_map/ppermute | solution.py:40
  348.3 1.0 copy-done.12
  349.3 23.5 %conv_back.1 = (bf16[256,4096]{1,0:T(8,128)(2,1)}, bf16[256,4096]{1,0:T(8,128)(2,1)}) custom-call(bf16[256,4096]{1,0:T(8,128)(2,1)} %get-tuple-element.17.grad_ref, bf16[128,4096]{1,0:T(8,128)(2,1)} %copy-done.12, bf16[256,4096]{1,0:T(8,128)(2,1)} %bitcast.26, bf16[256,4096]{1,0:T(8,128)(2,1)} %bitcast.28, f32[256,256]{1,0:T(8,128)} %concatenate.7.base_ref, ...), custom_call_target="tpu_custom_call" | custom-call | flops 4294967296 | bytes 12582912 | tf_op jit(solution)/shard_map/conv_back/pallas_call | solution.py:281
  372.8 1.5 multiply_convert_fusion.3
  374.4 57.7 %all-reduce.6.cloned.1.call-done = f32[64,1024]{1,0:T(8,128)} async-done(((f32[64,1024]{1,0:T(8,128)}), f32[64,1024]{1,0:T(8,128)}) %all-reduce.6.cloned.1.call-update) | async-done | bytes 262160 | tf_op jit(solution)/shard_map/psum | solution.py:420
  432.1 1.6 multiply_convert_fusion.2
  (19 shorter events, 0.0 us)
Async XLA Ops:
  7.2 7.9 %copy-start.5 = (bf16[256,128]{1,0:T(8,128)(2,1)S(1)}, bf16[256,128]{1,0:T(8,128)(2,1)}, u32[]{:S(2)}) copy-start(bf16[256,128]{1,0:T(8,128)(2,1)} %param.18) | copy-start | bytes 196612
  7.2 8.1 %copy-start.7 = (bf16[64,1024]{1,0:T(8,128)(2,1)S(1)}, bf16[64,1024]{1,0:T(8,128)(2,1)}, u32[]{:S(2)}) copy-start(bf16[64,1024]{1,0:T(8,128)(2,1)} %param.21) | copy-start | bytes 393220
  7.2 16.2 %copy-start.2 = (bf16[1,256,4096]{2,1,0:T(8,128)(2,1)S(1)}, bf16[1,256,4096]{2,1,0:T(8,128)(2,1)}, u32[]{:S(2)}) copy-start(bf16[1,256,4096]{2,1,0:T(8,128)(2,1)} %param.14) | copy-start | bytes 6291460
  7.2 320.4 %reduce-scatter.3.cloned.1.call-start = ((), (), s32[]{:S(2)}) async-start(), calls=%async_computation.2 | async-start | bytes 1179648 | tf_op jit(solution)/shard_map/reduce_scatter | solution.py:417
  9.2 27.3 %collective-permute-start = (bf16[128,4096]{1,0:T(8,128)(2,1)S(1)}, bf16[128,4096]{1,0:T(8,128)(2,1)}, u32[]{:S(2)}, u32[]{:S(2)}) collective-permute-start(bf16[128,4096]{1,0:T(8,128)(2,1)S(1)} %fusion.4), channel_id=1, source_target_pairs={{0,1},{1,2},{2,3},{3,4},{4,5},{5,6},{6,7},{8,9},{9,10},{10,11},{11... | collective-permute-start | bytes 3145736 | tf_op jit(solution)/shard_map/ppermute | solution.py:40
  22.5 14.0 %copy-start.4 = (bf16[64,4096]{1,0:T(8,128)(2,1)}, bf16[64,4096]{1,0:T(8,128)(2,1)S(1)}, u32[]{:S(2)}) copy-start(bf16[64,4096]{1,0:T(8,128)(2,1)S(1)} %all_gather.6.up_ref) | copy-start | bytes 1572868
  24.0 36.1 %copy-start.9 = (bf16[256,64]{1,0:T(8,128)(2,1)}, bf16[256,64]{1,0:T(8,128)(2,1)S(1)}, u32[]{:S(2)}) copy-start(bf16[256,64]{1,0:T(8,128)(2,1)S(1)} %fusion.6.back_up_ref) | copy-start | bytes 98308
  60.1 3.2 copy-start.8
  60.2 3.4 copy-start.10
  60.2 3.4 copy-start.11
  63.3 265.1 %reduce-scatter.5.cloned.1.call-start = ((), (), s32[]{:S(2)}) async-start(), calls=%async_computation.4 | async-start | bytes 1310720 | tf_op jit(solution)/shard_map/reduce_scatter | solution.py:418
  70.3 226.1 %copy-start = (bf16[256,4096]{1,0:T(8,128)(2,1)S(1)}, bf16[256,4096]{1,0:T(8,128)(2,1)}, u32[]{:S(2)}) copy-start(bf16[256,4096]{1,0:T(8,128)(2,1)} %get-tuple-element.13.input_ref) | copy-start | bytes 6291460
  263.2 33.9 %copy-start.3 = (bf16[1,256,4096]{2,1,0:T(8,128)(2,1)S(1)}, bf16[1,256,4096]{2,1,0:T(8,128)(2,1)}, u32[]{:S(2)}) copy-start(bf16[1,256,4096]{2,1,0:T(8,128)(2,1)} %param.14) | copy-start | bytes 6291460
  296.4 2.3 copy-start.1
  297.1 1.6 copy-start.6
  298.7 74.1 %all-reduce.4.cloned.1.call-start = ((), (), s32[]{:S(2)}) async-start(), calls=%async_computation.3 | async-start | bytes 262144 | tf_op jit(solution)/shard_map/psum | solution.py:419
  326.3 22.0 %collective-permute-start.1 = (bf16[128,4096]{1,0:T(8,128)(2,1)S(1)}, bf16[128,4096]{1,0:T(8,128)(2,1)S(1)}, u32[]{:S(2)}, u32[]{:S(2)}) collective-permute-start(bf16[128,4096]{1,0:T(8,128)(2,1)S(1)} %slice.21), channel_id=1, source_target_pairs={{1,0},{2,1},{3,2},{4,3},{5,4},{6,5},{7,6},{9,8},{10,9},{11,10},{12... | collective-permute-start | bytes 3145736 | tf_op jit(solution)/shard_map/ppermute | solution.py:40
  327.7 104.4 %all-reduce.6.cloned.1.call-start = ((), (), s32[]{:S(2)}) async-start(), calls=%async_computation.5 | async-start | bytes 524288 | tf_op jit(solution)/shard_map/psum | solution.py:420
  348.3 1.0 copy-start.12
Sparse Core Ops, SparseCore 0:
  63.5 67.6 reduce-scatter.2
  298.8 23.0 reduce-scatter.4
  327.8 30.0 all-reduce.3
  361.5 70.5 all-reduce.5

commit v2 on v1

--- a/solution.py
+++ b/solution.py
@@ -49,8 +49,17 @@
     return (levels * absmax).astype(jnp.bfloat16)
 
 
-def gather_kernel(line, own_ref, all_ref, local_sem, recv, sib_recv, z_send, y_send, x_send, sib_send):
+def gather_kernel(
+    line, tail_ref, own_ref, down_ref, up_ref, cot_ref, query_ref, key_ref, value_ref, base_ref, skip_ref,
+    all_ref, gated_ref, input_ref, term_down_ref, term_up_ref, proj_ref, back_up_ref, down_out, up_out,
+    before, down_all, up_all, back_up, proj,
+    local_sem, recv, sib_recv, z_send, y_send, x_send, sib_send,
+    halo_send, halo_recv, down_send, down_recv, up_send, up_recv,
+):
     f, c = lax.axis_index("fsdp"), lax.axis_index("ctx")
+    n_f, n_c = up_all.shape[0], 2 * line
+    tile = pl.program_id(0)
+    last = pl.num_programs(0) - 1
     x, k, z, y = f // 2, f % 2, c // 2, c % 2
     half = own_ref.shape[0] // 2
     x_peer = (lax.rem(f + 2, 4), c)
@@ -106,8 +115,9 @@
                         @pl.when(z > 0)
                         def _():
                             along_z(h, zz, 0).start()
-                along_y(0, x, y, zz).start()
-                along_x(1, x, y, zz).start()
+                for h in (0, 1):
+                    along_y(h, x, y, zz).start()
+                    along_x(1 - h, x, y, zz).start()
                 for h in (0, 1):
                     to_sibling(h, x, y, zz).start()
 
@@ -115,8 +125,6 @@
         for zz, there, _ in places(step):
             @pl.when(there)
             def _():
-                along_x(0, x, y, zz).start()
-                along_y(1, x, y, zz).start()
                 arrived(0, x, 1 - y, zz)
                 along_x(0, x, 1 - y, zz).start()
                 arrived(1, 1 - x, y, zz)
@@ -135,40 +143,113 @@
                     arrived(1, other, 1 - y, zz)
                     to_sibling(1, other, 1 - y, zz).start()
 
-    mine = pltpu.make_async_copy(
-        own_ref, all_ref.at[f, pl.ds(c * (2 * half), 2 * half), :], local_sem
-    )
-    mine.start()
-    barrier = pltpu.get_barrier_semaphore()
-    for peer in (x_peer, y_peer, sibling):
-        pl.semaphore_signal(barrier, inc=1, device_id=peer, device_id_type=MESH)
-
-    @pl.when(z + 1 < line)
-    def _():
-        pl.semaphore_signal(barrier, inc=1, device_id=z_up, device_id_type=MESH)
-
-    @pl.when(z > 0)
-    def _():
-        pl.semaphore_signal(barrier, inc=1, device_id=z_down, device_id_type=MESH)
-
-    inside = jnp.logical_and(z > 0, z + 1 < line)
-
-    @pl.when(inside)
-    def _():
-        pl.semaphore_wait(barrier, 5)
-
-    @pl.when(jnp.logical_not(inside))
-    def _():
-        pl.semaphore_wait(barrier, 4)
-
-    mine.wait()
-    for step in range(line + 2):
+    own_rows = down_ref.shape[0]
+
+    def halo():
+        return pltpu.make_async_remote_copy(
+            src_ref=tail_ref, dst_ref=before, send_sem=halo_send, recv_sem=halo_recv,
+            device_id=(f, c + 1), device_id_type=MESH,
+        )
+
+    def down_copy(turn, origin):
+        return pltpu.make_async_remote_copy(
+            src_ref=down_ref, dst_ref=down_all.at[pl.ds(origin * own_rows, own_rows)],
+            send_sem=down_send.at[turn], recv_sem=down_recv.at[origin],
+            device_id=(f, lax.rem(c + turn, n_c)), device_id_type=MESH,
+        )
+
+    def up_copy(turn, origin):
+        return pltpu.make_async_remote_copy(
+            src_ref=up_ref, dst_ref=up_all.at[origin],
+            send_sem=up_send.at[turn], recv_sem=up_recv.at[origin],
+            device_id=(lax.rem(f + turn, n_f), c), device_id_type=MESH,
+        )
+
+    def advance(step):
         if step < line:
             first(step)
         if 1 <= step <= line:
             second(step - 1)
         if step >= 2:
             third(step - 2)
+
+    nt = (((1,), (1,)), ((), ()))
+    over_rows = (((0,), (0,)), ((), ()))
+
+    @pl.when(tile == 0)
+    def _():
+        mine = pltpu.make_async_copy(
+            own_ref, all_ref.at[f, pl.ds(c * (2 * half), 2 * half), :], local_sem
+        )
+        mine.start()
+        barrier = pltpu.get_barrier_semaphore()
+        for turn in range(1, n_c):
+            pl.semaphore_signal(
+                barrier, inc=1, device_id=(f, lax.rem(c + turn, n_c)), device_id_type=MESH
+            )
+        for turn in range(1, n_f):
+            pl.semaphore_signal(
+                barrier, inc=1, device_id=(lax.rem(f + turn, n_f), c), device_id_type=MESH
+            )
+        pl.semaphore_wait(barrier, n_c + n_f - 2)
+
+        @pl.when(c + 1 < n_c)
+        def _():
+            halo().start()
+
+        for turn in range(1, n_f):
+            up_copy(turn, f).start()
+        for turn in range(1, n_c):
+            down_copy(turn, c).start()
+        mine.wait()
+        advance(0)
+        up_all[f] = up_ref[...]
+        down_all[pl.ds(pl.multiple_of(c * own_rows, own_rows), own_rows)] = down_ref[...]
+        proj[...] = jnp.zeros_like(proj)
+        for turn in range(1, n_f):
+            up_copy(turn, lax.rem(f + turn, n_f)).wait_recv()
+        for turn in range(1, n_c):
+            down_copy(turn, lax.rem(c + turn, n_c)).wait_recv()
+        width = up_ref.shape[1]
+        partial = jnp.zeros(proj.shape, jnp.float32)
+        for g in range(n_f):
+            columns = slice(g * width, (g + 1) * width)
+            up_out[:, columns] = up_all[g]
+            partial = partial + lax.dot_general(
+                cot_ref[:, columns], up_all[g], nt, preferred_element_type=jnp.float32
+            )
+        back_up[...] = partial.astype(jnp.bfloat16)
+        back_up_ref[...] = partial.astype(jnp.bfloat16)
+        down_out[...] = down_all[...]
+
+        @pl.when(c > 0)
+        def _():
+            halo().wait_recv()
+
+        @pl.when(c == 0)
+        def _():
+            before[...] = jnp.zeros_like(before)
+
+    for step, when in ((1, 2), (2, 16)):
+        @pl.when(tile == when)
+        def _():
+            advance(step)
+
+    taps = base_ref.shape[1] // 2
+    lanes = pl.ds(pl.multiple_of(tile * LANES, LANES), LANES)
+    mixed = (key_ref[...].astype(jnp.float32) * value_ref[...].astype(jnp.float32)).astype(
+        jnp.bfloat16
+    )
+    joined = jnp.concatenate([before[:, lanes], mixed], 0)
+    windows = [joined[b * taps : (b + 2) * taps] for b in range(mixed.shape[0] // taps)]
+    gated = conv_blocks(base_ref[...], windows) + skip_ref[...] * mixed.astype(jnp.float32)
+    gated_ref[...] = gated
+    gated_input = (query_ref[...].astype(jnp.float32) * gated).astype(jnp.bfloat16)
+    input_ref[...] = gated_input
+    proj[...] += jnp.dot(gated_input, down_all[lanes], preferred_element_type=jnp.float32)
+    term_down_ref[...] = lax.dot_general(
+        gated_input, back_up[...], over_rows, preferred_element_type=jnp.float32
+    )
 
     def finish(zz, carry):
         for xx in (0, 1):
@@ -191,19 +272,82 @@
                 along_z(h, zz, 0).wait_send()
         return carry
 
-    lax.fori_loop(0, line, finish, 0)
-
-
-def gather_weight(piece, n_f, n_c):
+    @pl.when(tile == last)
+    def _():
+        rounded = proj[...].astype(jnp.bfloat16)
+        proj_ref[...] = rounded
+        term_up_ref[...] = lax.dot_general(
+            rounded, cot_ref[...], over_rows, preferred_element_type=jnp.float32
+        )
+        for step in range(3, line + 2):
+            advance(step)
+        lax.fori_loop(0, line, finish, 0)
+        for turn in range(1, n_f):
+            up_copy(turn, f).wait_send()
+        for turn in range(1, n_c):
+            down_copy(turn, c).wait_send()
+
+        @pl.when(c + 1 < n_c)
+        def _():
+            halo().wait_send()
+
+
+def gather_weight(tail, piece, down, up, cot, query, key, value, base, skip, n_f, n_c):
     rows, columns = piece.shape
     line = n_c // 2
     blocks = (2, 2, 2, line)
+    count, channels = query.shape
+    rank, width = up.shape
+    tiles = channels // LANES
+    held = pl.BlockSpec(memory_space=pltpu.VMEM)
+    tile = pl.BlockSpec((count, LANES), lambda i: (0, i))
+    whole = lambda *shape: pl.BlockSpec(shape, lambda i: (0, 0))
+    shape = jax.ShapeDtypeStruct
+    half = jnp.bfloat16
+    full = jnp.float32
     return pl.pallas_call(
         functools.partial(gather_kernel, line),
-        out_shape=jax.ShapeDtypeStruct((n_f, n_c * rows, columns), piece.dtype),
-        in_specs=[pl.BlockSpec(memory_space=pl.ANY)],
-        out_specs=pl.BlockSpec(memory_space=pl.ANY),
+        grid=(tiles,),
+        out_shape=[
+            shape((n_f, n_c * rows, columns), half),
+            shape((count, channels), full),
+            shape((count, channels), half),
+            shape((channels, rank), full),
+            shape((rank, n_f * width), full),
+            shape((count, rank), half),
+            shape((count, rank), half),
+            shape((channels, rank), half),
+            shape((rank, n_f * width), half),
+        ],
+        in_specs=[
+            held,
+            pl.BlockSpec(memory_space=pl.ANY),
+            held,
+            held,
+            whole(*cot.shape),
+            tile,
+            tile,
+            tile,
+            pl.BlockSpec((base.shape[0] // tiles, base.shape[1]), lambda i: (i, 0)),
+            pl.BlockSpec((1, LANES), lambda i: (0, i)),
+        ],
+        out_specs=[
+            pl.BlockSpec(memory_space=pl.ANY),
+            tile,
+            tile,
+            pl.BlockSpec((LANES, rank), lambda i: (i, 0)),
+            whole(rank, n_f * width),
+            whole(count, rank),
+            whole(count, rank),
+            whole(channels, rank),
+            whole(rank, n_f * width),
+        ],
         scratch_shapes=[
+            pltpu.VMEM(tail.shape, half),
+            pltpu.VMEM((channels, rank), half),
+            pltpu.VMEM((n_f, rank, width), half),
+            pltpu.VMEM((count, rank), half),
+            pltpu.VMEM((count, rank), full),
             pltpu.SemaphoreType.DMA,
             pltpu.SemaphoreType.DMA(blocks),
             pltpu.SemaphoreType.DMA(blocks),
@@ -211,6 +355,12 @@
             pltpu.SemaphoreType.DMA(blocks),
             pltpu.SemaphoreType.DMA(blocks),
             pltpu.SemaphoreType.DMA(blocks),
+            pltpu.SemaphoreType.DMA,
+            pltpu.SemaphoreType.DMA,
+            pltpu.SemaphoreType.DMA((n_c,)),
+            pltpu.SemaphoreType.DMA((n_c,)),
+            pltpu.SemaphoreType.DMA((n_f,)),
+            pltpu.SemaphoreType.DMA((n_f,)),
         ],
         compiler_params=pltpu.CompilerParams(
             collective_id=0, has_side_effects=True, vmem_limit_bytes=VMEM_LIMIT
@@ -219,7 +369,7 @@
             flops=0, bytes_accessed=16 * n_f * n_c * rows * columns, transcendentals=0
         ),
         name="gather_weight",
-    )(piece)
+    )(tail, piece, down, up, cot, query, key, value, base, skip)
 
 
 def conv_blocks(base, windows):
@@ -244,18 +394,6 @@
             chosen = jnp.where(lanes == g, part[g * taps : (g + 1) * taps], chosen)
         results.append(chosen)
     return jnp.concatenate(results, 0)
-
-
-def ahead_kernel(query_ref, key_ref, value_ref, before_ref, base_ref, skip_ref, gated_ref, input_ref):
-    taps = base_ref.shape[1] // 2
-    mixed = (key_ref[...].astype(jnp.float32) * value_ref[...].astype(jnp.float32)).astype(
-        jnp.bfloat16
-    )
-    joined = jnp.concatenate([before_ref[...], mixed], 0)
-    windows = [joined[b * taps : (b + 2) * taps] for b in range(mixed.shape[0] // taps)]
-    gated = conv_blocks(base_ref[...], windows) + skip_ref[...] * mixed.astype(jnp.float32)
-    gated_ref[...] = gated
-    input_ref[...] = (query_ref[...].astype(jnp.float32) * gated).astype(jnp.bfloat16)
 
 
 def back_kernel(grad_ref, after_ref, key_ref, value_ref, base_ref, skip_ref, gk_ref, gv_ref):
@@ -388,36 +526,23 @@
     mixed_tail = (
         key[tail:].astype(jnp.float32) * value[tail:].astype(jnp.float32)
     ).astype(jnp.bfloat16)
-    before = from_behind(mixed_tail, "ctx", 1)
     piece = dequantize(quantized_weight_codes, scale_code_bytes, row_scale_second)
-    up = lax.all_gather(adapter_up_weight, "fsdp", axis=1, tiled=True)
-    down = lax.all_gather(adapter_down_weight, "ctx", axis=0, tiled=True)
     taps = filters.astype(jnp.float32)
     zeros = jnp.zeros((groups, filter_len), jnp.float32)
     back_base = jnp.concatenate([taps, zeros], 1)
     ahead_base = jnp.concatenate([zeros[:, :1], jnp.flip(taps, 1), zeros[:, 1:]], 1)
 
-    weight = gather_weight(piece, n_f, n_c)
-    gated, gated_input = tile_call(
-        ahead_kernel,
-        (query, key, value, before, ahead_base, skip),
-        (jnp.float32, jnp.bfloat16),
-        groups,
-        "conv_ahead",
-    )
-    back_up = lax.dot_general(
-        cot, up, (((1,), (1,)), ((), ())), preferred_element_type=jnp.float32
-    ).astype(jnp.bfloat16)
-    proj = jnp.dot(gated_input, down, preferred_element_type=jnp.float32).astype(jnp.bfloat16)
-    over_rows = (((0,), (0,)), ((), ()))
-    term_down = lax.dot_general(
-        gated_input, back_up, over_rows, preferred_element_type=jnp.float32
-    )
-    term_up = lax.dot_general(proj, cot, over_rows, preferred_element_type=jnp.float32)
+    weight, gated, gated_input, term_down, term_up, proj, back_up, down, up = gather_weight(
+        mixed_tail, piece, adapter_down_weight, adapter_up_weight, cot, query, key, value,
+        ahead_base, skip, n_f, n_c,
+    )
+    part_up = lax.psum_scatter(term_up, "fsdp", scatter_dimension=1, tiled=True)
     part_down = lax.psum_scatter(term_down, "ctx", scatter_dimension=0, tiled=True)
-    part_up = lax.psum_scatter(term_up, "fsdp", scatter_dimension=1, tiled=True)
     grad_down = multiplier * lax.psum(part_down, "fsdp")
-    grad_up = multiplier * lax.psum(part_up, "ctx")
+    part_up = lax.psum_scatter(part_up, "ctx", scatter_dimension=0, tiled=True)
+    grad_up = lax.all_gather(
+        (multiplier * part_up).astype(jnp.bfloat16), "ctx", axis=0, tiled=True
+    )
 
     output, grad_query, grad_gated = products(
         weight, cot, gated_input, gated, query, back_up, down, proj, up

time: 444 us -> 473 us (1.065)
  waiting for transfers between devices: 90.1 us -> 170 us
  Pallas kernels: 266 us -> 235 us
  blocking collectives: 40.3 us -> 30.5 us
  matrix products: 6.05 us -> 0 us
  starting transfers between devices: 7.31 us -> 1.45 us
    reduce_scatter x1, waiting for transfers between devices: 0.02 us -> 71.4 us  [local(): lax.psum_scatter(term_down, 'ctx', scatter_dimension=0, tiled=True)]
    reduce_scatter x0 -> x1, waiting for transfers between devices: none -> 62.7 us  [local(): part_up = lax.psum_scatter(part_up, 'ctx', scatter_dimension=0, tiled=True)]
    psum x1 -> x0, waiting for transfers between devices: 57.7 us -> none  [local(): grad_up = multiplier * lax.psum(part_up, 'ctx')]
    ppermute x2 -> x1, waiting for transfers between devices: 32.3 us -> 0.01 us  [from_behind(): return lax.ppermute(shard, axis, pairs)]
    reduce_scatter x1, waiting for transfers between devices: 0.01 us -> 25.6 us  [local(): part_up = lax.psum_scatter(term_up, 'fsdp', scatter_dimension=1, tiled=True)]
    pallas_call x2 -> x1, Pallas kernels: 47.2 us -> 23.5 us  [tile_call(): pl.pallas_call(kernel, grid=(tiles,), in_specs=[spec(a) for a in operands...]
    psum x1, waiting for transfers between devices: 0.01 us -> 9.95 us  [local(): grad_down = multiplier * lax.psum(part_down, 'fsdp')]
    all_gather x2 -> x1, blocking collectives: 40.3 us -> 30.5 us  [local(): lax.all_gather((multiplier * part_up).astype(jnp.bfloat16), 'ctx', axis=0...]
  transfers between devices with their start and end apart: 6 -> 5, of which waited for: 3 -> 4; matrix products, arithmetic and copies ran while one was open for 3% -> 1% of each run, Pallas kernels for 55% -> 11%
where the time goes in v2:
time: 473 us; the launch traced here: 469 us
  Pallas kernels  235 us (50%)
  waiting for transfers between devices  170 us (36%)
  blocking collectives  30.5 us (6%)
  between operations  13.8 us (3%)
  other arithmetic  9.04 us (2%)
  local copies, waits for them, and re-layouts  8.94 us (2%)
    pallas_call x1, Pallas kernels, gather_weight(): pl.pallas_call(functools.partial(gather_kernel, line), grid=(tiles,), out...  185 us
    reduce_scatter x1, waiting for transfers between devices, local(): lax.psum_scatter(term_down, 'ctx', scatter_dimension=0, tiled=True)  71.4 us
    reduce_scatter x1, waiting for transfers between devices, local(): part_up = lax.psum_scatter(part_up, 'ctx', scatter_dimension=0, tiled=True)  62.7 us
    all_gather x1, blocking collectives, local(): lax.all_gather((multiplier * part_up).astype(jnp.bfloat16), 'ctx', axis=0...  30.5 us
    pallas_call x1, Pallas kernels, products(): pl.pallas_call(product_kernel, grid=(channels // block,), in_specs=[pl.Bl...  26.3 us
    reduce_scatter x1, waiting for transfers between devices, local(): part_up = lax.psum_scatter(term_up, 'fsdp', scatter_dimension=1, tiled=True)  25.6 us
    pallas_call x1, Pallas kernels, tile_call(): pl.pallas_call(kernel, grid=(tiles,), in_specs=[spec(a) for a in operands...  23.5 us
    psum x1, waiting for transfers between devices, local(): grad_down = multiplier * lax.psum(part_down, 'fsdp')  9.95 us
  transfers between devices with their start and end apart: 5, of which 4 were waited for; matrix products, arithmetic and copies ran while one was open for 1% of the time, Pallas kernels for 11%

profile of v2, /device:TPU:0, one launch (start us, length us, event | category | flops | bytes accessed | tf_op | source)
XLA Modules:
  0.0 469.1 jit_solution(12471487613063007513)
XLA Ops:
  7.2 0.0 reduce-scatter.4.cloned.1.call-start
  7.2 0.8 multiply_multiply_fusion
  8.0 1.6 broadcast_in_dim.86
  9.6 0.0 copy-start.2
  9.6 0.0 copy-start.3
  9.6 2.0 copy.20
  11.5 0.0 copy-done.2
  11.5 0.2 rev.4
  11.7 0.1 pad.3.clone
  11.8 0.0 copy-done.3
  11.8 0.8 copy.21.down_ref
  12.6 0.0 copy-start
  12.6 0.0 copy-start.1
  12.6 4.5 multiply_convert_fusion.own_ref
  17.1 0.0 copy-done
  17.1 0.0 copy-done.1
  17.1 1.2 fusion.tail_ref
  18.3 0.8 maximum_maximum_fusion.base_ref
  19.1 185.1 %gather_weight.1 = (bf16[4,4096,1024]{2,1,0:T(8,128)(2,1)}, f32[256,4096]{1,0:T(8,128)}, bf16[256,4096]{1,0:T(8,128)(2,1)}, f32[4096,64]{1,0:T(8,128)}, f32[64,4...) custom-call(bf16[128,4096]{1,0:T(8,128)(2,1)} %fusion.tail_ref, ...), custom_call_target="tpu_custom_call" | custom-call | bytes 268435456 | tf_op jit(solution)/shard_map/gather_weight/pallas_call | solution.py:308
  204.2 0.0 reduce-scatter.4.cloned.1.call-update
  204.2 0.0 reduce-scatter.6.cloned.1.call-start
  204.3 0.7 reduce-scatter.6.cloned.1.call-update
  205.0 0.0 all-reduce.3.cloned.1.call-start
  205.0 26.3 %products.1 = (bf16[256,4096]{1,0:T(8,128)(2,1)}, bf16[256,4096]{1,0:T(8,128)(2,1)}, bf16[256,4096]{1,0:T(8,128)(2,1)}) custom-call(bf16[4,4096,1024]{2,1,0:T(8,128)(2,1)} %get-tuple-element.20.weight_ref, bf16[256,4096]{1,0:T(8,128)(2,1)} %bitcast.19, bf16[256,4096]{1,0:T(8,128)(2,1)} %get-tuple-element.21.input_ref, ...), custom_call_target="tpu_custom_call" | custom-call | flops 17179869184 | bytes 33554432 | tf_op jit(solution)/shard_map/products/pallas_call | solution.py:473
  231.3 1.3 slice.21
  232.6 1.3 collective-permute-start
  233.9 71.4 %reduce-scatter.4.cloned.1.call-done = f32[512,64]{1,0:T(8,128)} async-done(((f32[4096,64]{1,0:T(8,128)}), f32[512,64]{1,0:T(8,128)}) %reduce-scatter.4.cloned.1.call-update) | async-done | bytes 131088 | tf_op jit(solution)/shard_map/reduce_scatter | solution.py:540
  305.3 0.0 all-reduce.3.cloned.1.call-update
  305.3 0.0 reduce-scatter.8.cloned.1.call-start
  305.3 0.7 concatenate.7.base_ref
  306.1 25.6 %reduce-scatter.6.cloned.1.call-done = f32[64,1024]{1,0:T(8,128)} async-done(((f32[64,4096]{1,0:T(8,128)}), f32[64,1024]{1,0:T(8,128)}) %reduce-scatter.6.cloned.1.call-update) | async-done | bytes 262160 | tf_op jit(solution)/shard_map/reduce_scatter | solution.py:539
  331.7 0.0 reduce-scatter.8.cloned.1.call-update
  331.7 0.0 collective-permute-done.after_ref
  331.7 0.0 copy-start.4
  331.8 1.0 copy-done.4
  332.7 23.5 %conv_back.1 = (bf16[256,4096]{1,0:T(8,128)(2,1)}, bf16[256,4096]{1,0:T(8,128)(2,1)}) custom-call(bf16[256,4096]{1,0:T(8,128)(2,1)} %get-tuple-element.29.grad_ref, bf16[128,4096]{1,0:T(8,128)(2,1)} %copy-done.4, bf16[256,4096]{1,0:T(8,128)(2,1)} %bitcast.17, bf16[256,4096]{1,0:T(8,128)(2,1)} %bitcast.15, f32[256,256]{1,0:T(8,128)} %concatenate.7.base_ref, ...), custom_call_target="tpu_custom_call" | custom-call | flops 4294967296 | bytes 12582912 | tf_op jit(solution)/shard_map/conv_back/pallas_call | solution.py:419
  356.2 10.0 %all-reduce.3.cloned.1.call-done = f32[512,64]{1,0:T(8,128)} async-done(((f32[512,64]{1,0:T(8,128)}), f32[512,64]{1,0:T(8,128)}) %all-reduce.3.cloned.1.call-update) | async-done | bytes 131088 | tf_op jit(solution)/shard_map/psum | solution.py:541
  366.2 1.0 multiply_convert_fusion.2
  367.1 0.7 copy.22
  367.9 62.7 %reduce-scatter.8.cloned.1.call-done = f32[8,1024]{1,0:T(8,128)} async-done(((f32[64,1024]{1,0:T(8,128)}), f32[8,1024]{1,0:T(8,128)}) %reduce-scatter.8.cloned.1.call-update) | async-done | bytes 32784 | tf_op jit(solution)/shard_map/reduce_scatter | solution.py:542
  430.6 0.8 multiply_convert_fusion.3
  431.4 30.5 %all_gather.3 = bf16[64,1024]{1,0:T(8,128)(2,1)S(1)} all-gather(bf16[8,1024]{1,0:T(8,128)(2,1)S(1)} %multiply_convert_fusion.3), channel_id=1, replica_groups=mesh['fsdp'=4,'ctx'=8] {'ctx'}, dimensions={0}, use_global_device_ids=true | all-gather | bytes 147456 | tf_op jit(solution)/shard_map/all_gather | solution.py:543
  461.9 0.7 copy.25
  (2 shorter events, 0.0 us)
Async XLA Ops:
  7.2 298.1 %reduce-scatter.4.cloned.1.call-start = ((), (), s32[]{:S(2)}) async-start(), calls=%async_computation.3 | async-start | bytes 2359296 | tf_op jit(solution)/shard_map/reduce_scatter | solution.py:540
  9.6 2.0 copy-start.2
  9.6 2.2 copy-start.3
  12.6 4.5 copy-start
  12.6 4.5 copy-start.1
  204.2 127.5 %reduce-scatter.6.cloned.1.call-start = ((), (), s32[]{:S(2)}) async-start(), calls=%async_computation.5 | async-start | bytes 1310720 | tf_op jit(solution)/shard_map/reduce_scatter | solution.py:539
  205.0 161.2 %all-reduce.3.cloned.1.call-start = ((), (), s32[]{:S(2)}) async-start(), calls=%async_computation.4 | async-start | bytes 524288 | tf_op jit(solution)/shard_map/psum | solution.py:541
  232.6 99.2 %collective-permute-start = (bf16[128,4096]{1,0:T(8,128)(2,1)S(1)}, bf16[128,4096]{1,0:T(8,128)(2,1)S(1)}, u32[]{:S(2)}, u32[]{:S(2)}) collective-permute-start(bf16[128,4096]{1,0:T(8,128)(2,1)S(1)} %slice.21), channel_id=1, source_target_pairs={{1,0},{2,1},{3,2},{4,3},{5,4},{6,5},{7,6},{9,8},{10,9},{11,10},{12... | collective-permute-start | bytes 3145736 | tf_op jit(solution)/shard_map/ppermute | solution.py:40
  305.3 125.3 %reduce-scatter.8.cloned.1.call-start = ((), (), s32[]{:S(2)}) async-start(), calls=%async_computation.6 | async-start | bytes 294912 | tf_op jit(solution)/shard_map/reduce_scatter | solution.py:542
  331.7 1.0 copy-start.4
Sparse Core Ops, SparseCore 0:
  204.3 100.8 reduce-scatter.3
  307.8 23.8 reduce-scatter.5
  334.2 31.9 all-reduce.2
  369.3 61.2 reduce-scatter.7

commit v3 on v2

--- a/solution.py
+++ b/solution.py
@@ -50,11 +50,13 @@
 
 
 def gather_kernel(
-    line, tail_ref, own_ref, down_ref, up_ref, cot_ref, query_ref, key_ref, value_ref, base_ref, skip_ref,
-    all_ref, gated_ref, input_ref, term_down_ref, term_up_ref, proj_ref, back_up_ref, down_out, up_out,
+    line, multiplier, tail_ref, own_ref, down_ref, up_ref, cot_ref, query_ref, key_ref, value_ref, base_ref, skip_ref, back_base_ref,
+    all_ref, gated_ref, input_ref, grad_down_ref, grad_up_ref, proj_ref, back_up_ref, down_out, up_out, toep_ref,
     before, down_all, up_all, back_up, proj,
+    term_down, term_up, down_parts, up_parts, down_sum, down_sums, up_pieces, up_sums, up_whole,
     local_sem, recv, sib_recv, z_send, y_send, x_send, sib_send,
     halo_send, halo_recv, down_send, down_recv, up_send, up_recv,
+    send_1, recv_1, send_2, recv_2, send_3, recv_3, send_4, recv_4, send_5, recv_5,
 ):
     f, c = lax.axis_index("fsdp"), lax.axis_index("ctx")
     n_f, n_c = up_all.shape[0], 2 * line
@@ -164,6 +166,42 @@
             send_sem=up_send.at[turn], recv_sem=up_recv.at[origin],
             device_id=(lax.rem(f + turn, n_f), c), device_id_type=MESH,
         )
+
+    def pushes(on_ctx, source, target, send, arrive, incoming=False):
+        count, me = (n_c, c) if on_ctx else (n_f, f)
+        for turn in range(1, count):
+            peer = lax.rem(me + turn, count)
+            origin = peer if incoming else me
+            yield pltpu.make_async_remote_copy(
+                src_ref=source(peer), dst_ref=target.at[origin],
+                send_sem=send.at[turn], recv_sem=arrive.at[origin],
+                device_id=(f, peer) if on_ctx else (peer, c), device_id_type=MESH,
+            )
+
+    def rows_of(peer):
+        return term_down.at[pl.ds(pl.multiple_of(peer * own_rows, own_rows), own_rows)]
+
+    sums = (
+        (True, rows_of, down_parts, send_1, recv_1),
+        (False, lambda peer: term_up.at[peer], up_parts, send_2, recv_2),
+        (False, lambda peer: down_sum, down_sums, send_3, recv_3),
+        (True, lambda peer: up_pieces.at[peer], up_sums, send_4, recv_4),
+        (True, lambda peer: up_whole.at[c], up_whole, send_5, recv_5),
+    )
+
+    def begin(number):
+        for push in pushes(*sums[number]):
+            push.start()
+
+    def await_parts(number):
+        for push in pushes(*sums[number], incoming=True):
+            push.wait_recv()
+
+    def total_of(parts):
+        result = parts[0]
+        for number in range(1, parts.shape[0]):
+            result = result + parts[number]
+        return result
 
     def advance(step):
         if step < line:
@@ -235,6 +273,7 @@
         def _():
             advance(step)
 
+    toep_ref[...] = toeplitz(back_base_ref[...])
     taps = base_ref.shape[1] // 2
     lanes = pl.ds(pl.multiple_of(tile * LANES, LANES), LANES)
     mixed = (key_ref[...].astype(jnp.float32) * value_ref[...].astype(jnp.float32)).astype(
@@ -242,12 +281,12 @@
     )
     joined = jnp.concatenate([before[:, lanes], mixed], 0)
     windows = [joined[b * taps : (b + 2) * taps] for b in range(mixed.shape[0] // taps)]
-    gated = conv_blocks(base_ref[...], windows) + skip_ref[...] * mixed.astype(jnp.float32)
+    gated = conv_blocks(toeplitz(base_ref[...]), windows) + skip_ref[...] * mixed.astype(jnp.float32)
     gated_ref[...] = gated
     gated_input = (query_ref[...].astype(jnp.float32) * gated).astype(jnp.bfloat16)
     input_ref[...] = gated_input
     proj[...] += jnp.dot(gated_input, down_all[lanes], preferred_element_type=jnp.float32)
-    term_down_ref[...] = lax.dot_general(
+    term_down[lanes] = lax.dot_general(
         gated_input, back_up[...], over_rows, preferred_element_type=jnp.float32
     )
 
@@ -276,11 +315,43 @@
     def _():
         rounded = proj[...].astype(jnp.bfloat16)
         proj_ref[...] = rounded
-        term_up_ref[...] = lax.dot_general(
-            rounded, cot_ref[...], over_rows, preferred_element_type=jnp.float32
-        )
-        for step in range(3, line + 2):
+        width = up_ref.shape[1]
+        for g in range(n_f):
+            term_up[g] = lax.dot_general(
+                rounded, cot_ref[:, g * width : (g + 1) * width], over_rows,
+                preferred_element_type=jnp.float32,
+            )
+        begin(0)
+        begin(1)
+        down_parts[c] = rows_of(c)[...]
+        up_parts[f] = term_up[f]
+        advance(3)
+        await_parts(0)
+        await_parts(1)
+        down_sum[...] = total_of(down_parts)
+        down_sums[f] = down_sum[...]
+        up_mine = total_of(up_parts)
+        piece = up_mine.shape[0] // n_c
+        for g in range(n_c):
+            up_pieces[g] = up_mine[g * piece : (g + 1) * piece]
+        begin(2)
+        begin(3)
+        up_sums[c] = up_pieces[c]
+        for step in range(4, line + 1):
             advance(step)
+        await_parts(2)
+        await_parts(3)
+        grad_down_ref[...] = (multiplier * total_of(down_sums)).astype(jnp.bfloat16)
+        up_whole[c] = multiplier * total_of(up_sums)
+        begin(4)
+        advance(line + 1)
+        await_parts(4)
+        grad_up_ref[...] = jnp.concatenate(
+            [up_whole[g] for g in range(n_c)], 0
+        ).astype(jnp.bfloat16)
+        for group in sums:
+            for push in pushes(*group):
+                push.wait_send()
         lax.fori_loop(0, line, finish, 0)
         for turn in range(1, n_f):
             up_copy(turn, f).wait_send()
@@ -292,7 +363,7 @@
             halo().wait_send()
 
 
-def gather_weight(tail, piece, down, up, cot, query, key, value, base, skip, n_f, n_c):
+def gather_weight(tail, piece, down, up, cot, query, key, value, base, skip, back_base, n_f, n_c, multiplier):
     rows, columns = piece.shape
     line = n_c // 2
     blocks = (2, 2, 2, line)
@@ -306,18 +377,19 @@
     half = jnp.bfloat16
     full = jnp.float32
     return pl.pallas_call(
-        functools.partial(gather_kernel, line),
+        functools.partial(gather_kernel, line, multiplier),
         grid=(tiles,),
         out_shape=[
             shape((n_f, n_c * rows, columns), half),
             shape((count, channels), full),
             shape((count, channels), half),
-            shape((channels, rank), full),
-            shape((rank, n_f * width), full),
+            shape((rows, rank), half),
+            shape((rank, width), half),
             shape((count, rank), half),
             shape((count, rank), half),
             shape((channels, rank), half),
             shape((rank, n_f * width), half),
+            shape((base.shape[0] * base.shape[1] // 2, base.shape[1]), half),
         ],
         in_specs=[
             held,
@@ -330,17 +402,21 @@
             tile,
             pl.BlockSpec((base.shape[0] // tiles, base.shape[1]), lambda i: (i, 0)),
             pl.BlockSpec((1, LANES), lambda i: (0, i)),
+            pl.BlockSpec((base.shape[0] // tiles, base.shape[1]), lambda i: (i, 0)),
         ],
         out_specs=[
             pl.BlockSpec(memory_space=pl.ANY),
             tile,
             tile,
-            pl.BlockSpec((LANES, rank), lambda i: (i, 0)),
-            whole(rank, n_f * width),
+            whole(rows, rank),
+            whole(rank, width),
             whole(count, rank),
             whole(count, rank),
             whole(channels, rank),
             whole(rank, n_f * width),
+            pl.BlockSpec(
+                (base.shape[0] // tiles * base.shape[1] // 2, base.shape[1]), lambda i: (i, 0)
+            ),
         ],
         scratch_shapes=[
             pltpu.VMEM(tail.shape, half),
@@ -348,6 +424,15 @@
             pltpu.VMEM((n_f, rank, width), half),
             pltpu.VMEM((count, rank), half),
             pltpu.VMEM((count, rank), full),
+            pltpu.VMEM((channels, rank), full),
+            pltpu.VMEM((n_f, rank, width), full),
+            pltpu.VMEM((n_c, rows, rank), full),
+            pltpu.VMEM((n_f, rank, width), full),
+            pltpu.VMEM((rows, rank), full),
+            pltpu.VMEM((n_f, rows, rank), full),
+            pltpu.VMEM((n_c, rank // n_c, width), full),
+            pltpu.VMEM((n_c, rank // n_c, width), full),
+            pltpu.VMEM((n_c, rank // n_c, width), full),
             pltpu.SemaphoreType.DMA,
             pltpu.SemaphoreType.DMA(blocks),
             pltpu.SemaphoreType.DMA(blocks),
@@ -361,7 +446,8 @@
             pltpu.SemaphoreType.DMA((n_c,)),
             pltpu.SemaphoreType.DMA((n_f,)),
             pltpu.SemaphoreType.DMA((n_f,)),
-        ],
+        ]
+        + [pltpu.SemaphoreType.DMA((n,)) for n in (n_c, n_f, n_f, n_c, n_c) for _ in range(2)],
         compiler_params=pltpu.CompilerParams(
             collective_id=0, has_side_effects=True, vmem_limit_bytes=VMEM_LIMIT
         ),
@@ -369,21 +455,25 @@
             flops=0, bytes_accessed=16 * n_f * n_c * rows * columns, transcendentals=0
         ),
         name="gather_weight",
-    )(tail, piece, down, up, cot, query, key, value, base, skip)
-
-
-def conv_blocks(base, windows):
-    filters_here, width = base.shape
-    taps = width // 2
-    toep = jnp.concatenate(
+    )(tail, piece, down, up, cot, query, key, value, base, skip, back_base)
+
+
+def toeplitz(base):
+    taps = base.shape[1] // 2
+    return jnp.concatenate(
         [
             pltpu.roll(
-                jnp.broadcast_to(base[g : g + 1], (taps, width)), 0, 1, stride=1, stride_axis=0
+                jnp.broadcast_to(base[g : g + 1], (taps, 2 * taps)), 0, 1, stride=1, stride_axis=0
             )
-            for g in range(filters_here)
+            for g in range(base.shape[0])
         ],
         0,
     ).astype(jnp.bfloat16)
+
+
+def conv_blocks(toep, windows):
+    taps = toep.shape[1] // 2
+    filters_here = toep.shape[0] // taps
     product = jnp.dot(toep, jnp.concatenate(windows, 1), preferred_element_type=jnp.float32)
     lanes = lax.broadcasted_iota(jnp.int32, (taps, LANES), 1) // (LANES // filters_here)
     results = []
@@ -396,12 +486,12 @@
     return jnp.concatenate(results, 0)
 
 
-def back_kernel(grad_ref, after_ref, key_ref, value_ref, base_ref, skip_ref, gk_ref, gv_ref):
-    taps = base_ref.shape[1] // 2
+def back_kernel(grad_ref, after_ref, key_ref, value_ref, toep_ref, skip_ref, gk_ref, gv_ref):
+    taps = toep_ref.shape[1] // 2
     grad = grad_ref[...]
     joined = jnp.concatenate([grad, after_ref[...]], 0)
     windows = [joined[b * taps : (b + 2) * taps] for b in range(grad.shape[0] // taps)]
-    grad_mixed = conv_blocks(base_ref[...], windows) + skip_ref[...] * grad.astype(jnp.float32)
+    grad_mixed = conv_blocks(toep_ref[...], windows) + skip_ref[...] * grad.astype(jnp.float32)
     gk_ref[...] = (grad_mixed * value_ref[...].astype(jnp.float32)).astype(jnp.bfloat16)
     gv_ref[...] = (grad_mixed * key_ref[...].astype(jnp.float32)).astype(jnp.bfloat16)
 
@@ -411,9 +501,8 @@
     tiles = channels // LANES
 
     def spec(array):
-        if array.shape[0] == groups:
-            if array.shape[1] != channels:
-                return pl.BlockSpec((groups // tiles, array.shape[1]), lambda i: (i, 0))
+        if array.shape[0] % groups == 0 and array.shape[1] != channels:
+            return pl.BlockSpec((array.shape[0] // tiles, array.shape[1]), lambda i: (i, 0))
         return pl.BlockSpec((array.shape[0], LANES), lambda i: (0, i))
 
     return pl.pallas_call(
@@ -532,25 +621,17 @@
     back_base = jnp.concatenate([taps, zeros], 1)
     ahead_base = jnp.concatenate([zeros[:, :1], jnp.flip(taps, 1), zeros[:, 1:]], 1)
 
-    weight, gated, gated_input, term_down, term_up, proj, back_up, down, up = gather_weight(
+    weight, gated, gated_input, grad_down, grad_up, proj, back_up, down, up, toep = gather_weight(
         mixed_tail, piece, adapter_down_weight, adapter_up_weight, cot, query, key, value,
-        ahead_base, skip, n_f, n_c,
-    )
-    part_up = lax.psum_scatter(term_up, "fsdp", scatter_dimension=1, tiled=True)
-    part_down = lax.psum_scatter(term_down, "ctx", scatter_dimension=0, tiled=True)
-    grad_down = multiplier * lax.psum(part_down, "fsdp")
-    part_up = lax.psum_scatter(part_up, "ctx", scatter_dimension=0, tiled=True)
-    grad_up = lax.all_gather(
-        (multiplier * part_up).astype(jnp.bfloat16), "ctx", axis=0, tiled=True
-    )
-
+        ahead_base, skip, back_base, n_f, n_c, multiplier,
+    )
     output, grad_query, grad_gated = products(
         weight, cot, gated_input, gated, query, back_up, down, proj, up
     )
     after = from_behind(grad_gated[:filter_len], "ctx", -1)
     grad_key, grad_value = tile_call(
         back_kernel,
-        (grad_gated, after, key, value, back_base, skip),
+        (grad_gated, after, key, value, toep, skip),
         (jnp.bfloat16, jnp.bfloat16),
         groups,
         "conv_back",
@@ -560,8 +641,8 @@
         grad_query[None],
         grad_key[None],
         grad_value[None],
-        grad_down.astype(jnp.bfloat16),
-        grad_up.astype(jnp.bfloat16),
+        grad_down,
+        grad_up,
     )
 
 

time: 473 us -> 328 us (0.69)
  waiting for transfers between devices: 170 us -> 21.7 us
  Pallas kernels: 235 us -> 281 us
  blocking collectives: 30.5 us -> 0 us
  between operations: 13.8 us -> 0.68 us
    reduce_scatter x3 -> x0, waiting for transfers between devices: 160 us -> none  [the longest x1 71.4 us: local(): lax.psum_scatter(term_down, 'ctx', scatter_dimension=0, tiled=True)]
    pallas_call x1, Pallas kernels: 185 us -> 228 us  [gather_weight(): pl.pallas_call(functools.partial(gather_kernel, line, multiplier), grid=(...]
    all_gather x1 -> x0, blocking collectives: 30.5 us -> none  [local(): lax.all_gather((multiplier * part_up).astype(jnp.bfloat16), 'ctx', axis=0...]
    ppermute x1, waiting for transfers between devices: 0.01 us -> 21.7 us  [from_behind(): return lax.ppermute(shard, axis, pairs)]
    psum x1 -> x0, waiting for transfers between devices: 9.95 us -> none  [local(): grad_down = multiplier * lax.psum(part_down, 'fsdp')]
  transfers between devices with their start and end apart: 5 -> 1, of which waited for: 4 -> 1; matrix products, arithmetic and copies ran while one was open for 1% -> 0% of each run, Pallas kernels for 11% -> 0%
where the time goes in v3:
time: 328 us; the launch traced here: 325 us
  Pallas kernels  281 us (86%)
  waiting for transfers between devices  21.7 us (7%)
  local copies, waits for them, and re-layouts  12.5 us (4%)
  other arithmetic  8.53 us (3%)
    pallas_call x1, Pallas kernels, gather_weight(): pl.pallas_call(functools.partial(gather_kernel, line, multiplier), grid=(...  228 us
    pallas_call x1, Pallas kernels, tile_call(): pl.pallas_call(kernel, grid=(tiles,), in_specs=[spec(a) for a in operands...  26.3 us
    pallas_call x1, Pallas kernels, products(): pl.pallas_call(product_kernel, grid=(channels // block,), in_specs=[pl.Bl...  26.2 us
    ppermute x1, waiting for transfers between devices, from_behind(): return lax.ppermute(shard, axis, pairs)  21.7 us
  transfers between devices with their start and end apart: 1, of which 1 were waited for; matrix products, arithmetic and copies ran while one was open for 0% of the time, Pallas kernels for 0%

profile of v3, /device:TPU:0, one launch (start us, length us, event | category | flops | bytes accessed | tf_op | source)
XLA Modules:
  0.0 325.3 jit_solution(14539030411929083829)
XLA Ops:
  0.6 0.9 rev.4
  1.5 1.6 concatenate.7.back_base_ref
  3.1 0.1 pad.3.clone
  3.2 1.6 copy.21.down_ref
  4.8 0.8 multiply_multiply_fusion
  5.6 1.6 broadcast_in_dim.86
  7.1 0.0 copy-start
  7.2 3.0 copy.20
  10.2 0.0 copy-done
  10.2 0.0 copy-start.1
  10.2 2.6 fusion.tail_ref
  12.8 0.0 copy-done.1
  12.8 4.3 %multiply_convert_fusion.own_ref = bf16[512,1024]{1,0:T(8,128)(2,1)} fusion(f32[512,1024]{1,0:T(8,128)S(1)} %copy-done.1, s32[512,1024]{1,0:T(8,128)} %param.15), kind=kLoop, calls=%fused_computation | loop fusion | flops 17825792 | bytes 5242880 | tf_op jit(solution)/shard_map/convert_element_type | solution.py:49
  17.1 0.8 maximum_maximum_fusion.base_ref
  18.0 228.0 %gather_weight.1 = (bf16[4,4096,1024]{2,1,0:T(8,128)(2,1)}, f32[256,4096]{1,0:T(8,128)}, bf16[256,4096]{1,0:T(8,128)(2,1)}, bf16[512,64]{1,0:T(8,128)(2,1)}, bf1...) custom-call(bf16[128,4096]{1,0:T(8,128)(2,1)} %fusion.tail_ref, ...), custom_call_target="tpu_custom_call" | custom-call | bytes 268435456 | tf_op jit(solution)/shard_map/gather_weight/pallas_call | solution.py:379
  246.0 26.2 %products.1 = (bf16[256,4096]{1,0:T(8,128)(2,1)}, bf16[256,4096]{1,0:T(8,128)(2,1)}, bf16[256,4096]{1,0:T(8,128)(2,1)}) custom-call(bf16[4,4096,1024]{2,1,0:T(8,128)(2,1)} %get-tuple-element.21.weight_ref, bf16[256,4096]{1,0:T(8,128)(2,1)} %bitcast.19, bf16[256,4096]{1,0:T(8,128)(2,1)} %get-tuple-element.22.input_ref, ...), custom_call_target="tpu_custom_call" | custom-call | flops 17179869184 | bytes 33554432 | tf_op jit(solution)/shard_map/products/pallas_call | solution.py:562
  272.2 0.0 copy-start.3
  272.2 1.3 slice.21
  273.6 1.3 collective-permute-start
  274.9 0.0 copy-done.3
  274.9 0.7 copy.22
  275.6 21.7 %collective-permute-done.after_ref = bf16[128,4096]{1,0:T(8,128)(2,1)S(1)} collective-permute-done((bf16[128,4096]{1,0:T(8,128)(2,1)S(1)}, bf16[128,4096]{1,0:T(8,128)(2,1)S(1)}, u32[]{:S(2)}, u32[]{:S(2)}) %collective-permute-start) | collective-permute-done | bytes 1048608 | tf_op jit(solution)/shard_map/ppermute | solution.py:40
  297.3 0.0 copy-start.2
  297.3 1.0 copy-done.2
  298.3 0.0 copy-start.4
  298.3 26.3 %conv_back.1 = (bf16[256,4096]{1,0:T(8,128)(2,1)}, bf16[256,4096]{1,0:T(8,128)(2,1)}) custom-call(bf16[256,4096]{1,0:T(8,128)(2,1)} %get-tuple-element.30.grad_ref, bf16[128,4096]{1,0:T(8,128)(2,1)} %copy-done.2, bf16[256,4096]{1,0:T(8,128)(2,1)} %bitcast.16, bf16[256,4096]{1,0:T(8,128)(2,1)} %bitcast.14, bf16[32768,256]{1,0:T(8,128)(2,1)} %get-tuple-element.31.toep_ref, ...), custom_call_target="tpu_custom_call" | custom-call | flops 4294967296 | bytes 12582912 | tf_op jit(solution)/shard_map/conv_back/pallas_call | solution.py:508
  324.6 0.0 copy-done.4
  324.6 0.7 copy.24
  (2 shorter events, 0.0 us)
Async XLA Ops:
  7.1 3.0 copy-start
  10.2 2.6 copy-start.1
  272.2 2.6 copy-start.3
  273.6 23.8 %collective-permute-start = (bf16[128,4096]{1,0:T(8,128)(2,1)S(1)}, bf16[128,4096]{1,0:T(8,128)(2,1)S(1)}, u32[]{:S(2)}, u32[]{:S(2)}) collective-permute-start(bf16[128,4096]{1,0:T(8,128)(2,1)S(1)} %slice.21), channel_id=1, source_target_pairs={{1,0},{2,1},{3,2},{4,3},{5,4},{6,5},{7,6},{9,8},{10,9},{11,10},{12... | collective-permute-start | bytes 3145736 | tf_op jit(solution)/shard_map/ppermute | solution.py:40
  297.3 1.0 copy-start.2
  298.3 26.3 %copy-start.4 = (bf16[64,1024]{1,0:T(8,128)(2,1)S(1)}, bf16[64,1024]{1,0:T(8,128)(2,1)}, u32[]{:S(2)}) copy-start(bf16[64,1024]{1,0:T(8,128)(2,1)} %get-tuple-element.59) | copy-start | bytes 393220
